TPU v7x, 32 devices: a whole 2x2x4 slice. The times are simulated.
32 devices in a mesh: req: 4 (over y, x), exp: 8 (over z, core).
Axes of the slice: x: 2, y: 2, z: 4, core: 2. Of those that a mesh axis runs over, the one named last changes fastest.
Arguments:
- tokens: bfloat16 [8192, 1536], P(('req', 'exp')), may hold values from -6 to 6
- token_request_slot: int32 [32, 256], P(('req', 'exp')), may hold values from 0 to 3, never falling along the last dimension, each value on 1 to 128 neighbouring positions
- request_prompt: int32 [128], P(('req', 'exp')), may hold values from 0 to 7
- request_adapter: int32 [128], P(('req', 'exp')), may hold values from 0 to 15
- prompt_page_table: int32 [128], replicated, may hold values from 0 to 127, each once
- shared_prompt_cache: bfloat16 [128, 16, 512], P(('req', 'exp')), may hold values from -180 to 180
- routes: int32 [8192, 4], P(('req', 'exp')), may hold values from 0 to 7, all different within a row; in each aligned block of 256 rows (0 to 255, 256 to 511, ...) at most 192 rows name the same one
- attention_norm_gain: bfloat16 [1536], replicated, may hold values from 0.099609375 to 1.8984375
- query_matrix: bfloat16 [1536, 1536], replicated, may hold values from -0.15625 to 0.15625
- key_value_weight: bfloat16 [1536, 512], replicated, may hold values from -0.15625 to 0.15625
- attention_output_weight: bfloat16 [1536, 1536], replicated, may hold values from -0.15625 to 0.15625
- adapter_query_down: bfloat16 [1536, 256], replicated, may hold values from -0.15625 to 0.15625
- adapter_query_up: bfloat16 [256, 1536], replicated, may hold values from -1.5 to 1.5
- adapter_output_down: bfloat16 [1536, 256], replicated, may hold values from -0.15625 to 0.15625
- adapter_output_up: bfloat16 [256, 1536], replicated, may hold values from -1.5 to 1.5
- expert_norm_gain: bfloat16 [1536], replicated, may hold values from 0.099609375 to 1.8984375
- router: bfloat16 [1536, 8], replicated, may hold values from -0.15625 to 0.15625
- expert_gate_up: bfloat16 [8, 1536, 1536], P('exp'), may hold values from -0.15625 to 0.15625
- expert_down: bfloat16 [8, 768, 1536], P('exp'), may hold values from -0.21875 to 0.21875
Outputs:
- mixed_rows: bfloat16 [8192, 1536], P(('req', 'exp'))
Inputs may be any that keep to these rules, and one draw needn't show every extreme that they name: `token_request_slot`: along a device's row the slots never fall; each of the 4 slots holds 1 to 128 tokens and one holds exactly 128. `prompt_page_table`: the entries whose index divided by 16 (rounded down) is p are the pages of prompt p in order; every page appears once. `routes`: each token names 4 different experts. Among the tokens of one device no expert is named more than 192 times, and in every draw some device's tokens name some expert exactly 192 times.
All inputs are finite; a program needn't handle non-finite values.
Results may differ from a plain program's by a relative error of at most 0.017.
The roundings to bfloat16 on the way count: a program that leaves them out, or rounds other values in their place, can miss the bound.
Values may be sent and summed in bfloat16 or wider, within the bound.
No kernel may reach another device: no remote copies, remote signals or barrier semaphores. Data moves between devices by JAX's collectives and lax.ppermute only.
A program may use at most 128 MiB of HBM per device.

v0:
```python
import jax
import jax.numpy as jnp
from jax import lax
from jax.sharding import PartitionSpec as P

QUERY_HEADS = 12
KEY_VALUE_HEADS = 2
HEAD_WIDTH = 128
TOPK = 4
ADAPTER_RANK = 16
PPP = 16
PROMPT_LENGTH = 256


EPSILON = 1e-06
THETA = 1000000.0
VERY_NEGATIVE = -1e30


def rms_norm(weight_matrix, gain_vector):
    values = weight_matrix.astype(jnp.float32)
    factor = lax.rsqrt(jnp.mean(values * values, axis=-1, keepdims=True) + EPSILON)
    return (values * factor * gain_vector.astype(jnp.float32)).astype(jnp.bfloat16)


def apply_rotary(values, token_positions):
    half_width = values.shape[-1] // 2
    frequency = THETA ** (-jnp.arange(half_width).astype(jnp.float32) / half_width)
    angles = token_positions.astype(jnp.float32)[:, None] * frequency[None, :]
    cosine = jnp.cos(angles)[:, None, :]
    sine_table = jnp.sin(angles)[:, None, :]
    first_half = values[..., :half_width]
    second = values[..., half_width:]
    return jnp.concatenate(
        [first_half * cosine - second * sine_table, second * cosine + first_half * sine_table],
        axis=-1,
    )


def adapter_update(weight_matrix, down_proj, up_proj, token_adapter):
    inner = jnp.dot(weight_matrix, down_proj, preferred_element_type=jnp.float32)
    owner_slot = jnp.arange(down_proj.shape[1], dtype=jnp.int32) // ADAPTER_RANK
    inner = jnp.where(owner_slot[None, :] == token_adapter[:, None], inner, 0.0).astype(
        jnp.bfloat16
    )
    return jnp.dot(inner, up_proj, preferred_element_type=jnp.float32)


def request_info(request_row, prompt_req, adapter_req):
    new_token_count = request_row.shape[0]
    request_slot_count = prompt_req.shape[0]
    matches = request_row[:, None] == jnp.arange(request_slot_count, dtype=jnp.int32)[None, :]
    token_adapter = jnp.sum(jnp.where(matches, adapter_req[None, :], 0), axis=1)
    prompt_tok = jnp.sum(jnp.where(matches, prompt_req[None, :], 0), axis=1)
    token_index = jnp.arange(new_token_count, dtype=jnp.int32)
    first_row = jnp.min(jnp.where(matches, token_index[:, None], new_token_count), axis=0)
    start_tok = jnp.sum(jnp.where(matches, first_row[None, :], 0), axis=1)
    token_positions = PROMPT_LENGTH + token_index - start_tok
    return (token_adapter, prompt_tok, token_positions)


def apply_projection(
    tokens,
    token_adapter,
    token_positions,
    attention_norm_gain,
    query_matrix,
    key_value_weight,
    adapter_query_down,
    adapter_query_up,
):
    new_token_count = tokens.shape[0]
    normalized = rms_norm(tokens, attention_norm_gain)
    query_rows = jnp.dot(normalized, query_matrix, preferred_element_type=jnp.float32)
    query_rows = query_rows + adapter_update(
        normalized, adapter_query_down, adapter_query_up, token_adapter
    )
    query_rows = apply_rotary(
        query_rows.reshape(new_token_count, QUERY_HEADS, HEAD_WIDTH), token_positions
    ).astype(jnp.bfloat16)
    key_value_rows = jnp.dot(
        normalized, key_value_weight, preferred_element_type=jnp.float32
    ).reshape(new_token_count, 2 * KEY_VALUE_HEADS, HEAD_WIDTH)
    key_matrix = apply_rotary(key_value_rows[:, :KEY_VALUE_HEADS], token_positions).astype(
        jnp.bfloat16
    )
    value_matrix = key_value_rows[:, KEY_VALUE_HEADS:].astype(jnp.bfloat16)
    return (query_rows, key_matrix, value_matrix)


def finalize(
    attention_output,
    tokens,
    token_adapter,
    attention_output_weight,
    adapter_output_down,
    adapter_output_up,
):
    expert_mixture = jnp.dot(
        attention_output, attention_output_weight, preferred_element_type=jnp.float32
    )
    expert_mixture = expert_mixture + adapter_update(
        attention_output, adapter_output_down, adapter_output_up, token_adapter
    )
    return (tokens.astype(jnp.float32) + expert_mixture).astype(jnp.bfloat16)


def gate_weights(ffn_normed, router, routes):
    logits = jnp.dot(ffn_normed, router, preferred_element_type=jnp.float32)
    picked = jnp.take_along_axis(logits, routes, axis=1)
    squashed = jax.nn.sigmoid(picked)
    return squashed / jnp.sum(squashed, axis=1, keepdims=True)


def slot_of(routes, experts, capacity):
    flat_routes = routes.reshape(-1)
    onehot = (flat_routes[:, None] == jnp.arange(experts, dtype=jnp.int32)[None, :]).astype(
        jnp.int32
    )
    before = jnp.cumsum(onehot, axis=0) - onehot
    rank_pick = jnp.sum(before * onehot, axis=1)
    return flat_routes * capacity + rank_pick


def block_attention(running, grouped_queries, key_matrix, value_matrix, allowed):
    running_max, totals, accum = running
    scale = grouped_queries.shape[-1] ** (-0.5)
    scores = (
        jnp.einsum(
            "tkgd,nkd->tkgn", grouped_queries, key_matrix, preferred_element_type=jnp.float32
        )
        * scale
    )
    scores = jnp.where(allowed[:, None, None, :], scores, VERY_NEGATIVE)
    new_max = jnp.maximum(running_max, jnp.max(scores, axis=-1))
    factor = jnp.exp(running_max - new_max)
    weights = jnp.exp(scores - new_max[..., None])
    totals = totals * factor + jnp.sum(weights, axis=-1)
    summed = jnp.einsum(
        "tkgn,nkd->tkgd",
        weights.astype(jnp.bfloat16),
        value_matrix,
        preferred_element_type=jnp.float32,
    )
    accum = accum * factor[..., None] + summed
    return (new_max, totals, accum)


def on_device(
    tokens,
    token_request_slot,
    request_prompt,
    request_adapter,
    prompt_page_table,
    shared_prompt_cache,
    routes,
    attention_norm_gain,
    query_matrix,
    key_value_weight,
    attention_output_weight,
    adapter_query_down,
    adapter_query_up,
    adapter_output_down,
    adapter_output_up,
    expert_norm_gain,
    router,
    expert_gate_up,
    expert_down,
):
    new_token_count = tokens.shape[0]
    request_row = token_request_slot[0]
    request_slot_count = request_prompt.shape[0]
    token_adapter, prompt_tok, token_positions = request_info(
        request_row, request_prompt, request_adapter
    )
    query_rows, key_matrix, value_matrix = apply_projection(
        tokens,
        token_adapter,
        token_positions,
        attention_norm_gain,
        query_matrix,
        key_value_weight,
        adapter_query_down,
        adapter_query_up,
    )
    query_group_width = QUERY_HEADS // KEY_VALUE_HEADS
    grouped_queries = query_rows.reshape(
        new_token_count, KEY_VALUE_HEADS, query_group_width, HEAD_WIDTH
    )
    token_index = jnp.arange(new_token_count, dtype=jnp.int32)
    local_ok = (request_row[:, None] == request_row[None, :]) & (
        token_index[None, :] <= token_index[:, None]
    )
    initial = (
        jnp.full((new_token_count, KEY_VALUE_HEADS, query_group_width), VERY_NEGATIVE, jnp.float32),
        jnp.zeros((new_token_count, KEY_VALUE_HEADS, query_group_width), jnp.float32),
        jnp.zeros((new_token_count, KEY_VALUE_HEADS, query_group_width, HEAD_WIDTH), jnp.float32),
    )
    running_progress = block_attention(initial, grouped_queries, key_matrix, value_matrix, local_ok)
    requested_pages = jnp.take(prompt_page_table.reshape(-1, PPP), request_prompt, axis=0).reshape(
        -1
    )
    complete_cache = lax.all_gather(shared_prompt_cache, ("req", "exp"), axis=0, tiled=True)
    page_token_rows = jnp.take(complete_cache, requested_pages, axis=0).reshape(
        request_slot_count * PROMPT_LENGTH, 2 * KEY_VALUE_HEADS, HEAD_WIDTH
    )
    owner_slot = jnp.arange(request_slot_count * PROMPT_LENGTH, dtype=jnp.int32) // PROMPT_LENGTH
    prompt_valid_mask = request_row[:, None] == owner_slot[None, :]
    running_progress = block_attention(
        running_progress,
        grouped_queries,
        page_token_rows[:, :KEY_VALUE_HEADS],
        page_token_rows[:, KEY_VALUE_HEADS:],
        prompt_valid_mask,
    )
    running_max, totals, accum = running_progress
    attention_output = (
        (accum / totals[..., None])
        .reshape(new_token_count, QUERY_HEADS * HEAD_WIDTH)
        .astype(jnp.bfloat16)
    )
    hidden_state = finalize(
        attention_output,
        tokens,
        token_adapter,
        attention_output_weight,
        adapter_output_down,
        adapter_output_up,
    )
    ffn_normed = rms_norm(hidden_state, expert_norm_gain)
    gates = gate_weights(ffn_normed, router, routes)
    local_experts = expert_gate_up.shape[0]
    experts = local_experts * lax.axis_size("exp")
    capacity = 3 * new_token_count * TOPK // (2 * experts)
    destination = slot_of(routes, experts, capacity)
    slot_total = experts * capacity
    matches = jnp.arange(slot_total, dtype=jnp.int32)[:, None] == destination[None, :]
    source = jnp.arange(new_token_count * TOPK, dtype=jnp.int32) // TOPK
    source_tok = jnp.sum(jnp.where(matches, source[None, :], 0), axis=1)
    filled = jnp.any(matches, axis=1)
    outgoing = jnp.where(
        filled[:, None], jnp.take(ffn_normed, source_tok, axis=0), jnp.zeros((), jnp.bfloat16)
    )
    outgoing = outgoing.reshape(experts, capacity, -1)
    arrived = lax.all_to_all(outgoing, "exp", split_axis=0, concat_axis=0, tiled=True)
    sources = arrived.shape[0] // local_experts
    item_count = arrived.shape[1]
    arranged = arrived.reshape(sources, local_experts, item_count, -1)
    inner = jnp.einsum(
        "sxcd,xdf->sxcf", arranged, expert_gate_up, preferred_element_type=jnp.float32
    )
    half_width = inner.shape[-1] // 2
    units = (jax.nn.relu(inner[..., :half_width]) * inner[..., half_width:]).astype(jnp.bfloat16)
    result = jnp.einsum(
        "sxcf,xfd->sxcd", units, expert_down, preferred_element_type=jnp.float32
    ).astype(jnp.bfloat16)
    result = result.reshape(sources * local_experts, item_count, -1)
    returned = lax.all_to_all(result, "exp", split_axis=0, concat_axis=0, tiled=True)
    picked = jnp.take(returned.reshape(slot_total, -1), destination, axis=0).astype(jnp.float32)
    picked = picked.reshape(new_token_count, TOPK, -1)
    mixed_rows = hidden_state.astype(jnp.float32) + jnp.sum(gates[..., None] * picked, axis=1)
    return mixed_rows.astype(jnp.bfloat16)


def solution(mesh):
    return jax.shard_map(
        on_device,
        mesh=mesh,
        in_specs=(
            P(("req", "exp"), None),
            P(("req", "exp"), None),
            P(("req", "exp")),
            P(("req", "exp")),
            P(),
            P(("req", "exp"), None, None),
            P(("req", "exp"), None),
            P(),
            P(),
            P(),
            P(),
            P(),
            P(),
            P(),
            P(),
            P(),
            P(),
            P("exp", None, None),
            P("exp", None, None),
        ),
        out_specs=P(("req", "exp"), None),
        check_vma=False,
    )
```

profile of v0, /device:TPU:0, one launch (start us, length us, event | category | flops | bytes accessed | tf_op | source)
XLA Modules:
  0.0 385.4 jit_solution(4332308092321480788)
XLA Ops:
  24.3 3.1 fusion.75
  31.3 4.9 %fusion.73 = f32[256,1536]{1,0:T(8,128)} fusion(bf16[1536,1536]{1,0:T(8,128)(2,1)} %param.27, bf16[256,1536]{1,0:T(8,128)(2,1)S(1)} %copy-done.4, f32[1536]{0:T(1024)S(1)} %convert_element_type.85, f32[256]{0:T(256)S(1)} %add_rsqrt_fusion.1), kind=kOutput, calls=%fused_computation.158 | convolution fusion | flops 1209532416 | bytes 7085056 | tf_op jit(solution)/shard_map/dot_general | solution.py:74
  36.3 4.1 %convolution_add_fusion.1 = f32[256,1536]{1,0:T(8,128)} fusion(f32[256,1536]{1,0:T(8,128)} %fusion.73, bf16[256,1536]{1,0:T(8,128)(2,1)} %param.31, bf16[1536,256]{1,0:T(8,128)(2,1)} %param.30, s32[256]{0:T(256)S(1)} %and_select_fusion, s32[256]{0:T(256)S(1)} %get-tuple-element.5, bf16[256,1536]{1,0:T(8,128)(2,1)S(1)} %copy-done.4, ...), kind=kOutput, calls=%fused_computation.27 | convolution fusion | flops 404815872 | bytes 5514240 | tf_op jit(solution)/shard_map/dot_general | solution.py:46
  40.4 3.1 copy.94
  43.4 2.4 subtract_convert_fusion
  53.3 3.8 fusion.14
  57.1 12.5 %all-gather.2.cloned.1.call-done = bf16[128,16,512]{2,1,0:T(8,128)(2,1)} async-done(((bf16[4,16,512]{2,1,0:T(8,128)(2,1)}), bf16[128,16,512]{2,1,0:T(8,128)(2,1)}) %all-gather.2.cloned.1.call-update) | async-done | bytes 2097168 | tf_op jit(solution)/shard_map/all_gather | solution.py:203
  69.6 3.2 gather_fusion.1
  76.4 3.8 fusion.2
  83.2 2.5 fusion
  85.8 4.4 %fusion.25 = bf16[256,2,6,128]{0,3,2,1:T(8,128)(2,1)S(1)} fusion(f32[2,128,256,6]{2,1,3,0:T(8,128)} %fusion.22, f32[2,1024,256,6]{2,1,3,0:T(8,128)S(1)} %get-tuple-element.25, f32[256,2,6]{0,2,1:T(8,128)S(1)} %get-tuple-element.18, pred[256,1024]{0,1:T(8,128)(4,1)S(1)} %broadcast_compare_fusion, f32[256,2,6]{0,2,1:T(8,128)S(1)} %get-tuple-element.9, ...), kind=kOutput, calls=%fused_computation.44 | convolution fusion | flops 819855360 | bytes 15794176 | tf_op jit(solution)/shard_map/tkgn,nkd->tkgd/dot_general | solution.py:139
  91.1 5.0 %fusion.78 = f32[256,1536]{1,0:T(8,128)} fusion(bf16[256,1536]{0,1:T(8,128)(2,1)S(1)} %bitcast.125, bf16[1536,1536]{1,0:T(8,128)(2,1)} %param.29), kind=kOutput, calls=%fused_computation.161 | convolution fusion | flops 1207959552 | bytes 7077888 | tf_op jit(solution)/shard_map/dot_general | solution.py:99
  96.1 4.3 %multiply_reduce_fusion.1 = (f32[256]{0:T(256)S(1)}, f32[256,1536]{1,0:T(8,128)}) fusion(f32[256,1536]{1,0:T(8,128)} %fusion.78, bf16[256,1536]{1,0:T(8,128)(2,1)} %param.33, bf16[256,1536]{0,1:T(8,128)(2,1)} %bitcast.126, bf16[1536,256]{1,0:T(8,128)(2,1)} %param.32, s32[256]{0:T(256)S(1)} %copy-done.21, s32[256]{0:T(256)S(1)} %copy-done.17, ...), kind=kOutput, calls=%fused_computation.49 | convolution fusion | flops 405602048 | bytes 6294528 | tf_op jit(solution)/shard_map/dot_general | solution.py:46
  102.0 6.2 %gather_fusion.2 = bf16[1536,1536]{1,0:T(8,128)(2,1)} fusion(bf16[256,1536]{1,0:T(8,128)(2,1)S(1)} %multiply_convert_fusion, s32[2048]{0:T(1024)S(1)} %pad_clamp_fusion), kind=kCustom, calls=%fused_computation.2 | custom fusion | bytes 9443328 | tf_op jit(solution)/shard_map/jit(_take)/gather | solution.py:242
  108.3 2.9 select_select_fusion
  111.2 108.6 %all_to_all.10 = bf16[8,192,1536]{2,1,0:T(8,128)(2,1)S(1)} all-to-all(bf16[8,192,1536]{2,1,0:T(8,128)(2,1)S(1)} %select_select_fusion), channel_id=1, replica_groups=mesh['req'=4,'exp'=8] {'exp'}, dimensions={0} | all-to-all | bytes 9437184 | tf_op jit(solution)/shard_map/all_to_all | solution.py:245
  219.7 9.7 %convolution_bitcast_fusion = f32[8,1,192,1536]{3,2,0,1:T(8,128)S(1)} fusion(bf16[8,192,1536]{2,1,0:T(8,128)(2,1)S(1)} %all_to_all.10, bf16[1,1536,1536]{2,1,0:T(8,128)(2,1)} %param.36), kind=kOutput, calls=%fused_computation.16 | convolution fusion | flops 7247757312 | bytes 18874368 | tf_op jit(solution)/shard_map/sxcd,xdf->sxcf/dot_general | solution.py:249
  229.5 5.4 %convolution_convert_fusion = bf16[8,192,1536]{2,1,0:T(8,128)(2,1)} fusion(f32[8,1,192,1536]{3,2,0,1:T(8,128)S(1)} %convolution_bitcast_fusion, bf16[1,768,1536]{2,1,0:T(8,128)(2,1)S(1)} %copy-done), kind=kOutput, calls=%fused_computation.22 | convolution fusion | flops 3629776896 | bytes 16515072 | tf_op jit(solution)/shard_map/sxcf,xfd->sxcd/dot_general | solution.py:254
  234.9 4.7 %all-to-all-start.1 = ((bf16[8,192,1536]{2,1,0:T(8,128)(2,1)}), bf16[8,192,1536]{2,1,0:T(8,128)(2,1)}, u32[]{:S(2)}, u32[]{:S(2)}) async-start(bf16[8,192,1536]{2,1,0:T(8,128)(2,1)} %convolution_convert_fusion), calls=%async_computation.1 | async-start | bytes 9437184 | tf_op jit(solution)/shard_map/all_to_all | solution.py:258
  241.0 6.5 %gather_fusion.4 = f32[1024]{0:T(1024)S(1)} fusion(f32[256,8]{0,1:T(8,128)S(1)} %fusion.79, s32[1024]{0:T(1024)S(1)} %reshape.466), kind=kCustom, calls=%fused_computation.4 | custom fusion | bytes 16384 | tf_op jit(solution)/shard_map/jit(take_along_axis)/gather | solution.py:110
  248.0 97.0 %all-to-all-done.1 = bf16[8,192,1536]{2,1,0:T(8,128)(2,1)} async-done(((bf16[8,192,1536]{2,1,0:T(8,128)(2,1)}), bf16[8,192,1536]{2,1,0:T(8,128)(2,1)}, u32[]{:S(2)}, u32[]{:S(2)}) %all-to-all-start.1) | async-done | bytes 4718624 | tf_op jit(solution)/shard_map/all_to_all | solution.py:258
  344.9 10.2 %gather_fusion.3 = bf16[1024,1536]{1,0:T(8,128)(2,1)} fusion(bf16[1536,1536]{1,0:T(8,128)(2,1)} %bitcast.30, s32[1024]{0:T(1024)S(1)} %broadcast_clamp_fusion), kind=kCustom, calls=%fused_computation.3 | custom fusion | bytes 6295552 | tf_op jit(solution)/shard_map/jit(_take)/gather | solution.py:259
  355.1 6.1 %gather.33 = bf16[256,4,1536]{2,1,0:T(4,128)(2,1)} reshape(bf16[1024,1536]{1,0:T(8,128)(2,1)} %gather_fusion.3) | data formatting | bytes 6291456 | tf_op jit(solution)/shard_map/jit(_take)/gather | solution.py:259
  361.2 16.2 %multiply_reduce_fusion = f32[256,1536]{1,0:T(8,128)S(1)} fusion(bf16[256,4,1536]{2,1,0:T(4,128)(2,1)} %gather.33, f32[256,4]{1,0:T(8,128)S(1)} %copy.104, pred[256,4]{1,0:T(8,128)(4,1)S(1)} %copy.108), kind=kLoop, calls=%fused_computation.10 | loop fusion | flops 5898240 | bytes 4723712 | tf_op jit(solution)/shard_map/reduce_sum | solution.py:261
  (125 shorter events, 40.8 us)
Async XLA Ops:
  6.5 222.9 %copy-start = (bf16[1,768,1536]{2,1,0:T(8,128)(2,1)S(1)}, bf16[1,768,1536]{2,1,0:T(8,128)(2,1)}, u32[]{:S(2)}) copy-start(bf16[1,768,1536]{2,1,0:T(8,128)(2,1)} %param.37) | copy-start | bytes 7077892
  6.5 63.1 %all-gather.2.cloned.1.call-start = ((), (), s32[]{:S(2)}) async-start(), calls=%async_computation.2 | async-start | bytes 2162688 | tf_op jit(solution)/shard_map/all_gather | solution.py:203
  13.3 23.0 %copy-start.16 = (s32[256]{0:T(256)}, s32[256]{0:T(256)S(1)}, u32[]{:S(2)}) copy-start(s32[256]{0:T(256)S(1)} %get-tuple-element.5) | copy-start | bytes 3076
  19.7 11.6 %copy-start.13 = (s32[1536]{0:T(1024)}, s32[1536]{0:T(1024)S(1)}, u32[]{:S(2)}) copy-start(s32[1536]{0:T(1024)S(1)} %select_reduce_fusion) | copy-start | bytes 18436
  21.1 10.3 %copy-start.4 = (bf16[256,1536]{1,0:T(8,128)(2,1)S(1)}, bf16[256,1536]{1,0:T(8,128)(2,1)}, u32[]{:S(2)}) copy-start(bf16[256,1536]{1,0:T(8,128)(2,1)} %param.19) | copy-start | bytes 2359300
  21.4 14.9 %copy-start.7 = (f32[256,64]{0,1:T(8,128)}, f32[256,64]{0,1:T(8,128)S(1)}, u32[]{:S(2)}) copy-start(f32[256,64]{0,1:T(8,128)S(1)} %get-tuple-element.20) | copy-start | bytes 196612
  21.4 14.9 %copy-start.9 = (f32[256,64]{0,1:T(8,128)}, f32[256,64]{0,1:T(8,128)S(1)}, u32[]{:S(2)}) copy-start(f32[256,64]{0,1:T(8,128)S(1)} %get-tuple-element.21) | copy-start | bytes 196612
  31.3 4.9 %copy-start.20 = (s32[256]{0:T(256)}, s32[256]{0:T(256)S(1)}, u32[]{:S(2)}) copy-start(s32[256]{0:T(256)S(1)} %and_select_fusion) | copy-start | bytes 3076
  40.4 3.1 copy-start.8
  40.4 3.1 copy-start.10
  43.4 6.9 %copy-start.15 = (s32[1,256]{1,0:T(1,128)S(1)}, s32[1,256]{1,0:T(1,128)}, u32[]{:S(2)}) copy-start(s32[1,256]{1,0:T(1,128)} %param.20) | copy-start | bytes 3076
  57.1 17.9 %copy-start.19 = (pred[1024]{0:T(1024)(128)(4,1)S(1)}, pred[1024]{0:T(1024)(128)(4,1)}, u32[]{:S(2)}) copy-start(pred[1024]{0:T(1024)(128)(4,1)} %broadcast_in_dim.194) | copy-start | bytes 3076
  76.4 3.9 %copy-start.2 = (f32[2,256,256,6]{2,1,3,0:T(8,128)S(1)}, f32[2,256,256,6]{2,1,3,0:T(8,128)}, u32[]{:S(2)}) copy-start(f32[2,256,256,6]{2,1,3,0:T(8,128)} %get-tuple-element.23) | copy-start | bytes 9437188
  80.3 0.9 copy-start.11
  90.2 0.9 copy-start.6
  91.1 5.0 %copy-start.5 = (bf16[256,1536]{1,0:T(8,128)(2,1)S(1)}, bf16[256,1536]{1,0:T(8,128)(2,1)}, u32[]{:S(2)}) copy-start(bf16[256,1536]{1,0:T(8,128)(2,1)} %param.19) | copy-start | bytes 2359300
  91.1 5.0 %copy-start.17 = (s32[256]{0:T(256)S(1)}, s32[256]{0:T(256)}, u32[]{:S(2)}) copy-start(s32[256]{0:T(256)} %copy-done.16) | copy-start | bytes 3076
  91.1 5.0 %copy-start.21 = (s32[256]{0:T(256)S(1)}, s32[256]{0:T(256)}, u32[]{:S(2)}) copy-start(s32[256]{0:T(256)} %copy-done.20) | copy-start | bytes 3076
  102.0 6.2 %copy-start.18 = (pred[8,192]{1,0:T(8,128)(4,1)S(1)}, pred[8,192]{1,0:T(8,128)(4,1)}, u32[]{:S(2)}) copy-start(pred[8,192]{1,0:T(8,128)(4,1)} %broadcast_in_dim.200) | copy-start | bytes 4612
  234.9 4.9 %copy-start.12 = (s32[256,4]{0,1:T(4,128)S(1)}, s32[256,4]{0,1:T(4,128)}, u32[]{:S(2)}) copy-start(s32[256,4]{0,1:T(4,128)} %param.25) | copy-start | bytes 12292
  234.9 5.8 %copy-start.14 = (bf16[1536,8]{0,1:T(8,128)(2,1)S(1)}, bf16[1536,8]{0,1:T(8,128)(2,1)}, u32[]{:S(2)}) copy-start(bf16[1536,8]{0,1:T(8,128)(2,1)} %param.35) | copy-start | bytes 73732
  234.9 110.0 %all-to-all-start.1 = ((bf16[8,192,1536]{2,1,0:T(8,128)(2,1)}), bf16[8,192,1536]{2,1,0:T(8,128)(2,1)}, u32[]{:S(2)}, u32[]{:S(2)}) async-start(bf16[8,192,1536]{2,1,0:T(8,128)(2,1)} %convolution_convert_fusion), calls=%async_computation.1 | async-start | bytes 9437184 | tf_op jit(solution)/shard_map/all_to_all | solution.py:258
  361.2 16.3 %copy-start.3 = (f32[256,1536]{1,0:T(8,128)S(1)}, f32[256,1536]{1,0:T(8,128)}, u32[]{:S(2)}) copy-start(f32[256,1536]{1,0:T(8,128)} %get-tuple-element.27) | copy-start | bytes 4718596
  361.2 17.3 %copy-start.1 = (bf16[1,768,1536]{2,1,0:T(8,128)(2,1)S(1)}, bf16[1,768,1536]{2,1,0:T(8,128)(2,1)}, u32[]{:S(2)}) copy-start(bf16[1,768,1536]{2,1,0:T(8,128)(2,1)} %param.37) | copy-start | bytes 7077892
Sparse Core Ops, SparseCore 0:
  10.3 59.2 all-gather.1
where the time goes:
time: 387 us; the launch traced here: 385 us
  waiting for transfers between devices  110 us (28%)
  blocking collectives  109 us (28%)
  local copies, waits for them, and re-layouts  54.8 us (14%)
  matrix products  50.9 us (13%)
  other arithmetic  42.4 us (11%)
  between operations  13.8 us (4%)
  starting transfers between devices  4.72 us (1%)
    all_to_all x1, blocking collectives, on_device(): lax.all_to_all(outgoing, 'exp', split_axis=0, concat_axis=0, tiled=True)  109 us
    all_to_all x1, waiting for transfers between devices, on_device(): lax.all_to_all(result, 'exp', split_axis=0, concat_axis=0, tiled=True)  97 us
    gather x2, local copies, waits for them, and re-layouts, on_device(): jnp.take(returned.reshape(slot_total, -1), destination, axis=0)  16.3 us
    reduce_sum x1, other arithmetic, on_device(): jnp.sum(gates[..., None] * picked, axis=1)  16.2 us
    all_gather x1, waiting for transfers between devices, on_device(): lax.all_gather(shared_prompt_cache, ('req', 'exp'), axis=0, tiled=True)  12.5 us
    dot_general x1, matrix products, on_device(): jnp.einsum('sxcd,xdf->sxcf', arranged, expert_gate_up, preferred_element_...  9.72 us
    dot_general x2, matrix products, adapter_update(): return jnp.dot(inner, up_proj, preferred_element_type=jnp.float32)  8.44 us
  transfers between devices with their start and end apart: 2, of which 2 were waited for; matrix products, arithmetic and copies ran while one was open for 15% of the time, Pallas kernels for 0%

commit v1 on v0

v1 whole, which is shorter than its diff:
```python
import functools

import jax
import jax.numpy as jnp
from jax import lax
from jax.experimental import pallas as pl
from jax.experimental.pallas import tpu as pltpu
from jax.sharding import PartitionSpec as P

QUERY_HEADS = 12
KEY_VALUE_HEADS = 2
HEAD_WIDTH = 128
ADAPTER_RANK = 16
PPP = 16
PROMPT_LENGTH = 256
SEGMOST = 128
TILE = 64


EPSILON = 1e-06
LOG2_THETA = 19.931568569324174
VERY_NEGATIVE = -1e30
LOG2_E = 1.4426950408889634
MIB = 1 << 20

VMEM = pl.BlockSpec(memory_space=pltpu.VMEM)
SMEM = pl.BlockSpec(memory_space=pltpu.SMEM)
ANY = pl.BlockSpec(memory_space=pl.ANY)


def dot(one, other):
    return jnp.dot(one, other, preferred_element_type=jnp.float32)


def dot_transposed(one, other):
    return lax.dot_general(one, other, (((1,), (1,)), ((), ())), preferred_element_type=jnp.float32)


def rms_norm(values, gain):
    factor = lax.rsqrt(jnp.mean(values * values, axis=-1, keepdims=True) + EPSILON)
    return (values * factor * gain.astype(jnp.float32)).astype(jnp.bfloat16)


class Scalars:
    def __init__(self, ref, requests):
        self.starts = [ref[1 + slot] for slot in range(requests)]
        self.adapters = [ref[1 + requests + slot] for slot in range(requests)]
        self.place = lambda index: ref[1 + 2 * requests + index]

    def slot_of(self, row):
        return sum((row >= start).astype(jnp.int32) for start in self.starts[1:])


def prepare_kernel(
    pages_each, sizes, where, slots, prompts, adapters, page_table, numbers, outer
):
    requests = prompts.shape[0]
    exp_size, req_size = sizes
    exp, req = where[0], where[1]
    numbers[0] = exp
    held = slots[...]
    for slot in range(requests):
        numbers[1 + slot] = jnp.sum((held < slot).astype(jnp.int32))
        numbers[1 + requests + slot] = adapters[slot]

    def place(index, carry):
        page = page_table[prompts[index // PPP] * PPP + index % PPP]
        owner = page // pages_each
        apart = (owner % exp_size) ^ exp
        apart_req = (owner // exp_size) ^ req
        block = ((apart % 2) * req_size + apart_req) * (exp_size // 2) + apart // 2
        numbers[1 + 2 * requests + index] = block * pages_each + page % pages_each
        return carry

    lax.fori_loop(0, requests * PPP, place, 0)
    chip = exp // 2
    at_end = jnp.where((chip == 0) | (chip == 3), 1.0, 0.0)
    outer[...] = jnp.full(outer.shape, at_end, jnp.float32)


def by_slot(rows, starts, values):
    found = jnp.full(rows.shape, values[0], jnp.int32)
    for start, value in zip(starts[1:], values[1:]):
        found = jnp.where(rows >= start, value, found)
    return found


def own_columns(inner, adapter):
    column = lax.broadcasted_iota(jnp.int32, inner.shape, 1)
    return jnp.where(column // ADAPTER_RANK == adapter, inner, 0.0).astype(jnp.bfloat16)


def copies(pairs, semaphores):
    made = [
        pltpu.make_async_copy(source, target, semaphores.at[number])
        for number, (source, target) in enumerate(pairs)
    ]
    for copy in made:
        copy.start()
    return made


def projection_kernel(requests, routes_each, *refs):
    numbers, gain, tokens_there, query_matrix_there = refs[:4]
    key_value_weight_there, down_there, up_there = refs[4:7]
    blocks, refs = refs[7:-10], refs[-10:]
    query_rows, keys, values, named = refs[:4]
    tokens, query_matrix, key_value_weight, down, up, semaphores = refs[4:]
    chunks = query_matrix.shape[0]
    wide = query_matrix.shape[2]
    pairs = [
        (tokens_there, tokens),
        (key_value_weight_there, key_value_weight),
        (down_there, down),
        (up_there, up),
    ]
    for chunk in range(chunks):
        columns = pl.ds(chunk * wide, wide)
        pairs.append((query_matrix_there.at[:, columns], query_matrix.at[chunk]))
    got = copies(pairs, semaphores)
    scalars = Scalars(numbers, requests)
    count = tokens.shape[0]
    rows = lax.broadcasted_iota(jnp.int32, (count, 1), 0)
    adapter = by_slot(rows, scalars.starts, scalars.adapters)
    position = PROMPT_LENGTH + rows - by_slot(rows, scalars.starts, scalars.starts)
    lane = lax.broadcasted_iota(jnp.int32, (1, HEAD_WIDTH), 1) % (HEAD_WIDTH // 2)
    frequency = jnp.exp2(lane.astype(jnp.float32) * (-2.0 * LOG2_THETA / HEAD_WIDTH))
    angle = position.astype(jnp.float32) * frequency
    cosine, sine = jnp.cos(angle), jnp.sin(angle)
    lane = lax.broadcasted_iota(jnp.int32, angle.shape, 1)
    sine = jnp.where(lane < HEAD_WIDTH // 2, -sine, sine)

    def rotated(head):
        other = pltpu.roll(head, HEAD_WIDTH // 2, 1)
        return (head * cosine + other * sine).astype(jnp.bfloat16)

    named_rows = named.shape[1]
    expert = lax.broadcasted_iota(jnp.int32, (named.shape[2], named_rows), 0).astype(jnp.float32)
    for number, block in enumerate(blocks):
        page = block[block.shape[0] - 1].astype(jnp.float32)
        across = page.shape[1] // named_rows
        mentioned = jnp.zeros(expert.shape, jnp.float32)
        for k in range(routes_each):
            first = k % across * named_rows
            route = page[k // across : k // across + 1, first : first + named_rows]
            mentioned = jnp.where(expert == route, 1.0, mentioned)
        named[number] = mentioned.T
    got[0].wait()
    normed = rms_norm(tokens[...].astype(jnp.float32), gain[...][None, :])
    got[1].wait()
    key_value = dot(normed, key_value_weight[...])
    for head in range(KEY_VALUE_HEADS):
        lanes = slice(head * HEAD_WIDTH, (head + 1) * HEAD_WIDTH)
        keys[:, lanes] = rotated(key_value[:, lanes])
    values[...] = key_value[:, KEY_VALUE_HEADS * HEAD_WIDTH :].astype(jnp.bfloat16)
    got[2].wait()
    inner = own_columns(dot(normed, down[...]), adapter)
    got[3].wait()
    for chunk in range(chunks):
        got[4 + chunk].wait()
        first = chunk * wide
        part = dot(normed, query_matrix[chunk]) + dot(inner, up[:, first : first + wide])
        for head in range(wide // HEAD_WIDTH):
            lanes = slice(head * HEAD_WIDTH, (head + 1) * HEAD_WIDTH)
            query_rows[:, first + head * HEAD_WIDTH : first + (head + 1) * HEAD_WIDTH] = rotated(
                part[:, lanes]
            )


def fetch_kernel(requests, req_size, rows, *refs):
    numbers, gain, query_rows, keys, values, tokens = refs[:6]
    there = refs[6:13]
    parts = refs[13 : 13 + 2 * req_size]
    hidden, normed, prompt_rows, *held = refs[13 + 2 * req_size : -7]
    cache, attended, scratch, token_rows, part_semaphores, semaphores, token_semaphore = refs[-7:]
    pages = parts[0].shape[0]
    pairs = [
        (part, cache.at[pl.ds(number * pages, pages)]) for number, part in enumerate(parts)
    ]
    got_parts = copies(pairs, part_semaphores)
    got_tokens = copies([(tokens.at[pl.ds(0, rows)], token_rows)], token_semaphore)
    got = copies(list(zip(there, held)), semaphores)
    scalars = Scalars(numbers, requests)
    for copy in got_parts:
        copy.wait()

    def fetch(index, carry):
        prompt_rows[index] = cache[scalars.place(index)]
        return carry

    lax.fori_loop(0, requests * PPP, fetch, 0, unroll=4)
    attend(0, rows, scalars, query_rows, keys, values, prompt_rows, attended)
    for copy in got_tokens + got[:3]:
        copy.wait()
    project(0, scalars, gain, attended, token_rows, held[:3], hidden, normed, scratch)
    for copy in got[3:]:
        copy.wait()


def attention_kernel(requests, first_row, *refs):
    numbers, gain, query_rows, keys, values, tokens, prompt_rows, *weights = refs[:-6]
    hidden, normed, attended, scratch, token_rows, token_semaphore = refs[-6:]
    rows = token_rows.shape[0]
    got = copies([(tokens.at[pl.ds(first_row, rows)], token_rows)], token_semaphore)
    scalars = Scalars(numbers, requests)
    attend(first_row, rows, scalars, query_rows, keys, values, prompt_rows, attended)
    got[0].wait()
    project(first_row, scalars, gain, attended, token_rows, weights, hidden, normed, scratch)


def attend(first_row, count, scalars, query_rows, keys, values, prompt_rows, attended):
    starts = scalars.starts
    requests = len(starts)
    group = QUERY_HEADS // KEY_VALUE_HEADS
    factor = HEAD_WIDTH ** (-0.5) * LOG2_E
    for begin in range(first_row, first_row + count, TILE):
        end = begin + TILE
        window = max(0, begin - SEGMOST)
        rows = begin + lax.broadcasted_iota(jnp.int32, (TILE, 1), 0)
        columns = window + lax.broadcasted_iota(jnp.int32, (TILE, end - window), 1)
        row_slot = by_slot(rows, starts, list(range(requests)))
        row_start = by_slot(rows, starts, starts)
        blocked = jnp.where((columns >= row_start) & (columns <= rows), 0.0, VERY_NEGATIVE)
        blocked = jnp.concatenate([blocked] * group, axis=0)
        row_slot = jnp.concatenate([row_slot] * group, axis=0)
        lanes, value_lanes, grouped, state = [], [], [], []
        for head in range(KEY_VALUE_HEADS):
            lanes.append(slice(head * HEAD_WIDTH, (head + 1) * HEAD_WIDTH))
            place = KEY_VALUE_HEADS + head
            value_lanes.append(slice(place * HEAD_WIDTH, (place + 1) * HEAD_WIDTH))
            heads = range(head * group, (head + 1) * group)
            stacked = [query_rows[begin:end, h * HEAD_WIDTH : (h + 1) * HEAD_WIDTH] for h in heads]
            grouped.append(jnp.concatenate(stacked, axis=0))
        for head in range(KEY_VALUE_HEADS):
            scores = dot_transposed(grouped[head], keys[window:end, lanes[head]]) * factor + blocked
            largest = jnp.max(scores, axis=1, keepdims=True)
            weights = jnp.exp2(scores - largest)
            total = jnp.sum(weights, axis=1, keepdims=True)
            state.append(
                (largest, total, dot(weights.astype(jnp.bfloat16), values[window:end, lanes[head]]))
            )

        def add_prompt(slot, state):
            prompt_pages = prompt_rows[pl.ds(slot * PPP, PPP)]
            prompt = prompt_pages.reshape(PROMPT_LENGTH, prompt_pages.shape[-1])
            apart = jnp.where(row_slot == slot, 0.0, VERY_NEGATIVE)
            now = []
            for head in range(KEY_VALUE_HEADS):
                largest, total, summed = state[head]
                scores = dot_transposed(grouped[head], prompt[:, lanes[head]]) * factor + apart
                highest = jnp.maximum(largest, jnp.max(scores, axis=1, keepdims=True))
                weights = jnp.exp2(scores - highest)
                shrink = jnp.exp2(largest - highest)
                total = total * shrink + jnp.sum(weights, axis=1, keepdims=True)
                added = dot(weights.astype(jnp.bfloat16), prompt[:, value_lanes[head]])
                now.append((highest, total, summed * shrink + added))
            return tuple(now)

        state = lax.fori_loop(
            scalars.slot_of(begin), scalars.slot_of(end - 1) + 1, add_prompt, tuple(state)
        )
        for head in range(KEY_VALUE_HEADS):
            largest, total, summed = state[head]
            result = (summed / total).astype(jnp.bfloat16)
            for place in range(group):
                h = head * group + place
                attended[
                    begin - first_row : end - first_row, h * HEAD_WIDTH : (h + 1) * HEAD_WIDTH
                ] = result[place * TILE : (place + 1) * TILE]


def project(first_row, scalars, gain, attended, tokens, weights, hidden, normed, scratch):
    output_weight, down, up = weights
    count = tokens.shape[0]
    rows = first_row + lax.broadcasted_iota(jnp.int32, (count, 1), 0)
    adapter = by_slot(rows, scalars.starts, scalars.adapters)
    inner = own_columns(dot(attended[...], down[...]), adapter)
    width = tokens.shape[1]
    squares = jnp.zeros((count, 1), jnp.float32)
    for first in range(0, width, 512):
        columns = slice(first, first + 512)
        added = dot(attended[...], output_weight[:, columns]) + dot(inner, up[:, columns])
        part = (tokens[:, columns].astype(jnp.float32) + added).astype(jnp.bfloat16)
        hidden[:, columns] = part
        part = part.astype(jnp.float32)
        scratch[:, columns] = part
        squares = squares + jnp.sum(part * part, axis=1, keepdims=True)
    scale = lax.rsqrt(squares / width + EPSILON)
    wide = gain[...][None, :].astype(jnp.float32)
    normed[...] = (scratch[...] * scale * wide).astype(jnp.bfloat16)


def expert_kernel(plan, numbers, near, far, named, router, *refs):
    weights, (out, units) = refs[:4], refs[-2:]
    exp = numbers[0]
    chip = exp // 2
    use_near, owner, start = plan(chip)
    if use_near is None:
        rows = jnp.concatenate([near[...], far[...]], axis=0)
    else:
        rows = jnp.where(use_near, near[...], far[...])
    mentioned = named[chip ^ owner, pl.ds(start, rows.shape[0]), :]
    squashed = jnp.where(mentioned > 0.0, jax.nn.sigmoid(dot_transposed(rows, router[...])), 0.0)
    gates = squashed / jnp.sum(squashed, axis=1, keepdims=True)
    lane = lax.broadcasted_iota(jnp.int32, gates.shape, 1)
    hidden_units, width = weights[1].shape
    for number in range(2):
        gate_up = weights[2 * number]
        for first in range(0, hidden_units, 256):
            left = dot(rows, gate_up[:, first : first + 256])
            right = dot(rows, gate_up[:, hidden_units + first : hidden_units + first + 256])
            units[number, :, first : first + 256] = (jnp.maximum(left, 0.0) * right).astype(
                jnp.bfloat16
            )
    gate_columns = [
        jnp.sum(jnp.where(lane == (exp ^ number), gates, 0.0), axis=1, keepdims=True)
        for number in range(2)
    ]
    for first in range(0, width, 512):
        columns = slice(first, first + 512)
        total = 0.0
        for number in range(2):
            result = dot(units[number], weights[2 * number + 1][:, columns]).astype(jnp.bfloat16)
            total = total + gate_columns[number] * result.astype(jnp.float32)
        out[:, columns] = total.astype(out.dtype)


def call(kernel, inputs, specs, outs, scratch, name, flops, limit, out_specs=None):
    moved = sum(x.size * x.dtype.itemsize for x in inputs)
    return pl.pallas_call(
        kernel,
        in_specs=specs,
        out_specs=out_specs or [VMEM] * len(outs),
        out_shape=outs,
        scratch_shapes=scratch,
        name=name,
        cost_estimate=pl.CostEstimate(flops=flops, bytes_accessed=moved, transcendentals=0),
        compiler_params=pltpu.CompilerParams(vmem_limit_bytes=limit * MIB),
    )(*inputs)


def expert_sum(near, far, plan, shared, dtype, rows=None, earlier=()):
    numbers, named, router, weights = shared
    rows = near.shape[0] if rows is None else rows
    hidden_units, width = weights[1].shape
    return call(
        functools.partial(expert_kernel, plan),
        [numbers, near, far, named, router, *weights, *earlier],
        [SMEM] + [VMEM] * 8 + [ANY] * len(earlier),
        [jax.ShapeDtypeStruct((rows, width), dtype)],
        [pltpu.VMEM((2, rows, hidden_units), jnp.bfloat16)],
        "expert_sum",
        12 * rows * width * hidden_units,
        10,
    )[0]


def after(values, *earlier):
    return pl.pallas_call(
        lambda *refs: None,
        in_specs=[ANY] * (len(values) + len(earlier)),
        out_specs=[ANY] * len(values),
        out_shape=[jax.ShapeDtypeStruct(x.shape, x.dtype) for x in values],
        input_output_aliases={number: number for number in range(len(values))},
        name="after",
        compiler_params=pltpu.CompilerParams(vmem_limit_bytes=MIB),
    )(*values, *earlier)


def chosen_kernel(outer, for_outer, for_inner, *refs):
    refs[-1][...] = jnp.where(outer[0:1, 0:1] > 0.0, for_outer[...], for_inner[...])


def added_kernel(one, other, *refs):
    total = one[...].astype(jnp.float32) + other[...].astype(jnp.float32)
    refs[-1][...] = total.astype(jnp.bfloat16)


def payload(kernel, inputs, earlier):
    one = inputs[-1]
    return call(
        kernel,
        [*inputs, *earlier],
        [VMEM] * len(inputs) + [ANY] * len(earlier),
        [jax.ShapeDtypeStruct(one.shape, one.dtype)],
        [],
        "payload",
        one.size,
        2,
    )[0]


def swap(values, axis, distance):
    size = lax.axis_size(axis)
    return lax.ppermute(values, axis, [(i, i ^ distance) for i in range(size)])


def gather_line(values):
    chips = lax.axis_size("exp") // 2
    return [values] + [swap(values, "exp", 2 * distance) for distance in range(1, chips)]


def gather_plane(line):
    return [swap(line, "req", distance) for distance in range(1, lax.axis_size("req"))]


def next_chip(values):
    size = lax.axis_size("exp")
    return lax.ppermute(values, "exp", [(i, (i + 2) % size) for i in range(size)])


def ring_experts(halves, shared, outer_here):
    chips = lax.axis_size("exp") // 2
    own = jnp.concatenate(halves, axis=0)
    rows, partial = own, None
    for step in range(1, chips):
        rows = next_chip(rows)
        plan = lambda chip, step=step: (True, lax.rem(chip + (chips - step), chips), 0)
        part = expert_sum(rows, rows, plan, shared, jnp.float32)
        if partial is not None:
            part = part + next_chip(partial).astype(jnp.float32)
        partial = part.astype(jnp.bfloat16)
    total = expert_sum(own, own, lambda chip: (True, chip, 0), shared, jnp.float32)
    if partial is not None:
        total = total + next_chip(partial).astype(jnp.float32)
    return total


COMPUTED = {
    2: ((1, 2, 1, 2), (0, 0, 0, 0)),
    3: ((2, 3, 0, 1), (0, 0, 0, 0)),
    4: ((3, 3, 0, 0), (0, 1, 1, 0)),
    5: ((3, 2, 1, 0), (1, 1, 1, 1)),
    6: ((2, 0, 3, 1), (1, 0, 0, 1)),
    7: ((1, 0, 3, 2), (1, 1, 1, 1)),
}


def by_chip(chip, numbers):
    found = numbers[0]
    for other, number in enumerate(numbers[1:], 1):
        found = jnp.where(chip == other, number, found)
    return found


def line_experts(halves, shared, outer_here):
    size = lax.axis_size("exp")
    first, second = halves
    half = first.shape[0]
    inner_pairs = [(i, i ^ 6) for i in range(2, size - 2)]

    def chosen(for_outer, for_inner, *earlier):
        return payload(chosen_kernel, [outer_here, for_outer, for_inner], earlier)

    def added(one, other, *earlier):
        return payload(added_kernel, [one, other], earlier)

    side, middle, sums = {}, {}, {}

    def send_side(slot, *earlier):
        if slot == 2:
            rows = chosen(second, middle[1], *earlier)
        elif slot <= 5:
            rows = chosen(sums[slot - 1], middle[slot - 1], *earlier)
        elif slot == 6:
            rows = chosen(sums[5], second, middle[5], *earlier)
        else:
            rows = added(middle[slot - 1], sums[slot - 1], *earlier)
        side[slot] = swap(rows, "exp", 2)
        return rows

    def send_middle(slot, *earlier):
        if slot <= 3:
            rows = chosen(side[slot - 1], side[slot - 1], *earlier)
        elif slot == 4:
            rows = chosen(side[3], second, *earlier)
        else:
            rows = added(side[slot - 1], sums[slot - 3], *earlier)
        middle[slot] = lax.ppermute(rows, "exp", inner_pairs)
        return rows

    side[1] = swap(first, "exp", 2)
    middle[1] = lax.ppermute(first, "exp", inner_pairs)
    last = second
    for slot in range(2, 9):
        if slot % 2:
            sent = send_middle(slot, send_side(slot, last))
        else:
            sent = send_side(slot, send_middle(slot, last))
        if slot in COMPUTED:
            inner_rows = middle[slot - 1] if slot <= 5 else side[slot - 5]

            def plan(chip, slot=slot):
                owners, whichs = COMPUTED[slot]
                use_near = (chip == 0) | (chip == 3)
                start = pl.multiple_of(by_chip(chip, whichs) * half, half)
                return use_near, by_chip(chip, owners), start

            sums[slot] = expert_sum(side[slot - 1], inner_rows, plan, shared, jnp.bfloat16)
            last = sums[slot]
    plan = lambda chip: (None, chip, 0)
    total = expert_sum(first, second, plan, shared, jnp.float32, 2 * half, (sent,))
    back = chosen(side[7], side[3]).astype(jnp.float32) + middle[5].astype(jnp.float32)
    back_second = side[8].astype(jnp.float32) + middle[8].astype(jnp.float32)
    return total + jnp.concatenate([back, back_second], axis=0)


def on_device(
    tokens,
    token_request_slot,
    request_prompt,
    request_adapter,
    prompt_page_table,
    shared_prompt_cache,
    routes,
    attention_norm_gain,
    query_matrix,
    key_value_weight,
    attention_output_weight,
    adapter_query_down,
    adapter_query_up,
    adapter_output_down,
    adapter_output_up,
    expert_norm_gain,
    router,
    expert_gate_up,
    expert_down,
):
    count, width = tokens.shape
    requests = request_prompt.shape[0]
    experts = router.shape[1]
    other_gate_up = swap(expert_gate_up, "exp", 1)
    other_down = swap(expert_down, "exp", 1)
    page = shared_prompt_cache.shape[1:]
    pages_each = shared_prompt_cache.shape[0]
    where = jnp.stack([lax.axis_index("exp"), lax.axis_index("req")]).astype(jnp.int32)
    sizes = (lax.axis_size("exp"), lax.axis_size("req"))
    numbers, outer_here = call(
        functools.partial(prepare_kernel, pages_each, sizes),
        [where, token_request_slot, request_prompt, request_adapter, prompt_page_table],
        [SMEM, VMEM, SMEM, SMEM, SMEM],
        [
            jax.ShapeDtypeStruct((1 + 2 * requests + requests * PPP,), jnp.int32),
            jax.ShapeDtypeStruct((8, HEAD_WIDTH), jnp.float32),
        ],
        [],
        "prepare",
        count * width,
        4,
        [SMEM, VMEM],
    )
    route_rows = routes.T.reshape(-1, page[1]).astype(jnp.bfloat16)
    route_page = jnp.pad(route_rows, ((0, page[0] - route_rows.shape[0]), (0, 0)))
    blocks = gather_line(jnp.concatenate([shared_prompt_cache, route_page[None]], axis=0))
    line = jnp.concatenate([block[:pages_each] for block in blocks], axis=0)
    (line,) = after([line], outer_here)
    key_width = KEY_VALUE_HEADS * HEAD_WIDTH
    heads_width = query_matrix.shape[1]
    rank = adapter_query_down.shape[1]
    bfloat = lambda *shape: pltpu.VMEM(shape, jnp.bfloat16)
    query_rows, keys, values, named = call(
        functools.partial(projection_kernel, requests, routes.shape[1]),
        [
            numbers,
            attention_norm_gain,
            tokens,
            query_matrix,
            key_value_weight,
            adapter_query_down,
            adapter_query_up,
            *blocks,
        ],
        [SMEM, VMEM] + [ANY] * 5 + [VMEM] * len(blocks),
        [
            jax.ShapeDtypeStruct((count, columns), jnp.bfloat16)
            for columns in (heads_width, key_width, key_width)
        ]
        + [jax.ShapeDtypeStruct((len(blocks), count, experts), jnp.float32)],
        [
            bfloat(count, width),
            bfloat(heads_width // 512, width, 512),
            bfloat(width, 2 * key_width),
            bfloat(width, rank),
            bfloat(rank, heads_width),
            pltpu.SemaphoreType.DMA((4 + heads_width // 512,)),
        ],
        "projections",
        2 * count * width * (heads_width + 3 * key_width),
        52,
    )
    parts = after([line, *gather_plane(line)], keys)
    parts = [*parts] + [swap(part, "exp", 1) for part in parts]
    pages = len(parts) * parts[0].shape[0]
    half = count // 2
    rows_out = [jax.ShapeDtypeStruct((half, width), jnp.bfloat16)] * 2
    projected = [numbers, expert_norm_gain, query_rows, keys, values, tokens]
    output_weights = [attention_output_weight, adapter_output_down, adapter_output_up]
    weights = [expert_gate_up[0], expert_down[0], other_gate_up[0], other_down[0]]
    working = [
        bfloat(half, heads_width),
        pltpu.VMEM((half, width), jnp.float32),
        bfloat(half, width),
    ]
    hidden_first, first, prompt_rows, *held = call(
        functools.partial(fetch_kernel, requests, sizes[1], half),
        [*projected, *output_weights, *weights, *parts],
        [SMEM] + [VMEM] * 4 + [ANY] * (8 + len(parts)),
        rows_out
        + [bfloat(requests * PPP, *page)]
        + [bfloat(*weight.shape) for weight in output_weights + weights],
        [bfloat(pages, *page)]
        + working
        + [pltpu.SemaphoreType.DMA((number,)) for number in (len(parts), 7, 1)],
        "first_attention",
        2 * count * width * width,
        22,
    )
    hidden_second, second = call(
        functools.partial(attention_kernel, requests, half),
        [*projected, prompt_rows, *held[:3]],
        [SMEM] + [VMEM] * 4 + [ANY] + [VMEM] * 4,
        rows_out,
        working + [pltpu.SemaphoreType.DMA((1,))],
        "second_attention",
        2 * count * width * width,
        8,
    )
    hidden_state = jnp.concatenate([hidden_first, hidden_second], axis=0)
    halves, weights = (first, second), held[3:]
    experts_of = line_experts if lax.axis_size("exp") == 8 else ring_experts
    shared = (numbers, named, router.T, weights)
    mixed_rows = hidden_state.astype(jnp.float32) + experts_of(halves, shared, outer_here)
    return mixed_rows.astype(jnp.bfloat16)


def solution(mesh):
    return jax.shard_map(
        on_device,
        mesh=mesh,
        in_specs=(
            P(("req", "exp"), None),
            P(("req", "exp"), None),
            P(("req", "exp")),
            P(("req", "exp")),
            P(),
            P(("req", "exp"), None, None),
            P(("req", "exp"), None),
            P(),
            P(),
            P(),
            P(),
            P(),
            P(),
            P(),
            P(),
            P(),
            P(),
            P("exp", None, None),
            P("exp", None, None),
        ),
        out_specs=P(("req", "exp"), None),
        check_vma=False,
    )
```

time: 387 us -> 131 us (0.34)
  blocking collectives: 109 us -> 0 us
  waiting for transfers between devices: 110 us -> 23.7 us
  local copies, waits for them, and re-layouts: 54.8 us -> 2.71 us
  matrix products: 50.9 us -> 0 us
  starting transfers between devices: 4.72 us -> 54.5 us
  Pallas kernels: 0 us -> 45.9 us
  other arithmetic: 42.4 us -> 3.96 us
  between operations: 13.8 us -> 0.44 us
    all_to_all x1 -> x0, blocking collectives: 109 us -> none  [on_device(): lax.all_to_all(outgoing, 'exp', split_axis=0, concat_axis=0, tiled=True)]
    all_to_all x1 -> x0, waiting for transfers between devices: 97 us -> none  [on_device(): lax.all_to_all(result, 'exp', split_axis=0, concat_axis=0, tiled=True)]
    ppermute x0 -> x28, starting transfers between devices: none -> 54.5 us  [the longest x20 48.8 us: swap(): return lax.ppermute(values, axis, [(i, i ^ distance) for i in range(size)])]
    dot_general x12 -> x0, matrix products: 50.9 us -> none  [the longest x1 9.72 us: on_device(): jnp.einsum('sxcd,xdf->sxcf', arranged, expert_gate_up, preferred_element_...]
    pallas_call x0 -> x28, Pallas kernels: none -> 45.9 us  [the longest x26 45.9 us: call(): pl.pallas_call(kernel, in_specs=specs, out_specs=out_specs or [VMEM] * le...]
    gather x11 -> x0, local copies, waits for them, and re-layouts: 35.5 us -> none  [the longest x2 16.3 us: on_device(): jnp.take(returned.reshape(slot_total, -1), destination, axis=0)]
    ppermute x0 -> x28, waiting for transfers between devices: none -> 23.7 us  [the longest x20 23.7 us: swap(): return lax.ppermute(values, axis, [(i, i ^ distance) for i in range(size)])]
    reduce_sum x8 -> x0, other arithmetic: 22.4 us -> none  [the longest x1 16.2 us: on_device(): jnp.sum(gates[..., None] * picked, axis=1)]
  transfers between devices with their start and end apart: 2 -> 28, of which waited for: 2 -> 13; matrix products, arithmetic and copies ran while one was open for 15% -> 2% of each run, Pallas kernels for 0% -> 30%
where the time goes in v1:
time: 131 us
  starting transfers between devices  54.5 us (42%)
  Pallas kernels  45.9 us (35%)
  waiting for transfers between devices  23.7 us (18%)
  other arithmetic  3.96 us (3%)
  local copies, waits for them, and re-layouts  2.71 us (2%)
    ppermute x20, starting transfers between devices, swap(): return lax.ppermute(values, axis, [(i, i ^ distance) for i in range(size)])  48.8 us
    pallas_call x26, Pallas kernels, call(): pl.pallas_call(kernel, in_specs=specs, out_specs=out_specs or [VMEM] * le...  45.9 us
    ppermute x20, waiting for transfers between devices, swap(): return lax.ppermute(values, axis, [(i, i ^ distance) for i in range(size)])  23.7 us
    ppermute x7, starting transfers between devices, send_middle(): middle[slot] = lax.ppermute(rows, 'exp', inner_pairs)  5.02 us
    unnamed x22, local copies, waits for them, and re-layouts  2.67 us
  transfers between devices with their start and end apart: 28, of which 13 were waited for; matrix products, arithmetic and copies ran while one was open for 2% of the time, Pallas kernels for 30%

profile of v1, /device:TPU:0, one launch (start us, length us, event | category | flops | bytes accessed | tf_op | source)
XLA Modules:
  0.0 131.2 jit_solution(4403357474700937406)
XLA Ops:
  2.1 5.1 %collective-permute-start.2 = (bf16[5,16,512]{2,1,0:T(8,128)(2,1)S(1)}, bf16[5,16,512]{2,1,0:T(8,128)(2,1)S(1)}, u32[]{:S(2)}, u32[]{:S(2)}) collective-permute-start(bf16[5,16,512]{2,1,0:T(8,128)(2,1)S(1)} %pad_maximum_fusion.1.refs_7_), channel_id=1, source_target_pairs={{0,6},{1,7},{2,4},{3,5},{4,2},{5,3},{6,0},{7,1},{8,14},{9,15},{10,... | collective-permute-start | bytes 245768 | tf_op jit(solution)/shard_map/ppermute | solution.py:395
  10.5 3.6 %prepare.1 = (s32[73]{0:T(128)S(1)}, f32[8,128]{1,0:T(8,128)S(1)}) custom-call(s32[2]{0:T(128)S(1)} %pad_add_fusion.where, s32[1,256]{1,0:T(1,128)S(1)} %copy-done.7, s32[4]{0:T(128)S(1)} %copy-done.8, s32[4]{0:T(128)S(1)} %copy-done.9, s32[128]{0:T(128)S(1)} %copy-done.10), custom_call_target="tpu_custom_call" | custom-call | flops 393216 | bytes 1576 | tf_op jit(solution)/shard_map/prepare/pallas_call | solution.py:330
  15.2 2.6 %collective-permute-start.7 = (bf16[16,16,512]{2,1,0:T(8,128)(2,1)S(1)}, bf16[16,16,512]{2,1,0:T(8,128)(2,1)S(1)}, u32[]{:S(2)}, u32[]{:S(2)}) collective-permute-start(bf16[16,16,512]{2,1,0:T(8,128)(2,1)S(1)} %after.2.refs_0_), channel_id=1, source_target_pairs={{0,24},{8,16},{16,8},{24,0},{1,25},{9,17},{17,9},{25,1},{2,26},{10... | collective-permute-start | bytes 786440 | tf_op jit(solution)/shard_map/ppermute | solution.py:395
  18.8 7.4 %projections.1 = (bf16[256,1536]{1,0:T(8,128)(2,1)S(1)}, bf16[256,256]{1,0:T(8,128)(2,1)S(1)}, bf16[256,256]{1,0:T(8,128)(2,1)S(1)}, f32[4,256,8]{2,1,0:T(8,128)S(1)}) custom-call(s32[73]{0:T(128)S(1)} %get-tuple-element.27.refs_0_.numbers, bf16[1536]{0:T(1024)(128)(2,1)S(1)} %copy-done.6, bf16[256,1536]{1,0:T(8,128)(2,1)} %refs_5_.5, ...), custom_call_target="tpu_custom_call" | custom-call | flops 1811939328 | bytes 8981796 | tf_op jit(solution)/shard_map/projections/pallas_call | solution.py:330
  26.2 3.2 %collective-permute-done.6.refs_2_ = bf16[16,16,512]{2,1,0:T(8,128)(2,1)S(1)} collective-permute-done((bf16[16,16,512]{2,1,0:T(8,128)(2,1)S(1)}, bf16[16,16,512]{2,1,0:T(8,128)(2,1)S(1)}, u32[]{:S(2)}, u32[]{:S(2)}) %collective-permute-start.6) | collective-permute-done | bytes 262176 | tf_op jit(solution)/shard_map/ppermute | solution.py:395
  32.7 6.3 %first_attention.1 = (bf16[128,1536]{1,0:T(8,128)(2,1)S(1)}, bf16[128,1536]{1,0:T(8,128)(2,1)S(1)}, bf16[64,16,512]{2,1,0:T(8,128)(2,1)S(1)}, bf16[1536,1536]{1,...) custom-call(s32[73]{0:T(128)S(1)} %get-tuple-element.27.refs_0_.numb, ...), custom_call_target="tpu_custom_call" | custom-call | flops 1207959552 | bytes 24382756 | tf_op jit(solution)/shard_map/first_attention/pallas_call | solution.py:330
  42.2 6.9 %second_attention.1 = (bf16[128,1536]{1,0:T(8,128)(2,1)S(1)}, bf16[128,1536]{1,0:T(8,128)(2,1)S(1)}) custom-call(s32[73]{0:T(128)S(1)} %get-tuple-element.27.refs_0_.numbers, bf16[1536]{0:T(1024)(128)(2,1)S(1)} %copy-done.5, bf16[256,1536]{1,0:T(8,128)(2,1)S(1)} %get-tuple-element.28.refs_2_, bf16[256,256]{1,0:T(8,128)(2,1)S(1)} %get-tuple-element.29.refs_4_.refs_3_, ...), custom_call_target="tpu_custom_call" | custom-call | flops 1207959552 | bytes 9178404 | tf_op jit(solution)/shard_map/second_attention/pallas_call | solution.py:330
  52.1 4.1 %collective-permute-start.14 = (bf16[128,1536]{1,0:T(8,128)(2,1)S(1)}, bf16[128,1536]{1,0:T(8,128)(2,1)S(1)}, u32[]{:S(2)}, u32[]{:S(2)}) collective-permute-start(bf16[128,1536]{1,0:T(8,128)(2,1)S(1)} %payload.16), channel_id=1, source_target_pairs={{0,2},{1,3},{2,0},{3,1},{4,6},{5,7},{6,4},{7,5},{8,10},{9,11},{10,... | collective-permute-start | bytes 1179656 | tf_op jit(solution)/shard_map/ppermute | solution.py:395
  56.3 2.7 %expert_sum.8.for_outer.refs_0_.other = bf16[128,1536]{1,0:T(8,128)(2,1)S(1)} custom-call(s32[73]{0:T(128)S(1)} %get-tuple-element.27.refs_0_.numbers, bf16[128,1536]{1,0:T(8,128)(2,1)S(1)} %collective-permute-done.13.for_outer.for_inner.near.far, bf16[128,1536]{1,0:T(8,128)(2,1)S(1)} %collective-permute-done.12.for_inner.far, ...), custom_call_target="tpu_custom_call" | custom-call | flops 1811939328 | bytes 14999844 | tf_op jit(solution)/shard_map/expert_sum/pallas_call | solution.py:330
  59.0 7.2 %collective-permute-start.17 = (bf16[128,1536]{1,0:T(8,128)(2,1)S(1)}, bf16[128,1536]{1,0:T(8,128)(2,1)S(1)}, u32[]{:S(2)}, u32[]{:S(2)}) collective-permute-start(bf16[128,1536]{1,0:T(8,128)(2,1)S(1)} %payload.17.refs_0_), channel_id=1, source_target_pairs={{0,2},{1,3},{2,0},{3,1},{4,6},{5,7},{6,4},{7,5},{8,10},{9,11},{10,... | collective-permute-start | bytes 1179656 | tf_op jit(solution)/shard_map/ppermute | solution.py:395
  67.0 2.7 %expert_sum.7.refs_0_.for_outer.other = bf16[128,1536]{1,0:T(8,128)(2,1)S(1)} custom-call(s32[73]{0:T(128)S(1)} %get-tuple-element.27.refs_0_.numbers, bf16[128,1536]{1,0:T(8,128)(2,1)S(1)} %collective-permute-done.14.near.for_outer.for_inner.far, bf16[128,1536]{1,0:T(8,128)(2,1)S(1)} %collective-permute-done.15.far.for_inner, ...), custom_call_target="tpu_custom_call" | custom-call | flops 1811939328 | bytes 14999844 | tf_op jit(solution)/shard_map/expert_sum/pallas_call | solution.py:330
  69.6 5.9 %collective-permute-done.17.for_outer.near.for_inner = bf16[128,1536]{1,0:T(8,128)(2,1)S(1)} collective-permute-done((bf16[128,1536]{1,0:T(8,128)(2,1)S(1)}, bf16[128,1536]{1,0:T(8,128)(2,1)S(1)}, u32[]{:S(2)}, u32[]{:S(2)}) %collective-permute-start.17) | collective-permute-done | bytes 393248 | tf_op jit(solution)/shard_map/ppermute | solution.py:395
  76.5 3.0 %collective-permute-start.18 = (bf16[128,1536]{1,0:T(8,128)(2,1)S(1)}, bf16[128,1536]{1,0:T(8,128)(2,1)S(1)}, u32[]{:S(2)}, u32[]{:S(2)}) collective-permute-start(bf16[128,1536]{1,0:T(8,128)(2,1)S(1)} %payload.20), channel_id=1, source_target_pairs={{0,2},{1,3},{2,0},{3,1},{4,6},{5,7},{6,4},{7,5},{8,10},{9,11},{10,... | collective-permute-start | bytes 1179656 | tf_op jit(solution)/shard_map/ppermute | solution.py:395
  79.5 2.7 %expert_sum.10.for_outer.refs_0_.other = bf16[128,1536]{1,0:T(8,128)(2,1)S(1)} custom-call(s32[73]{0:T(128)S(1)} %get-tuple-element.27.refs_0_.numbers, bf16[128,1536]{1,0:T(8,128)(2,1)S(1)} %collective-permute-done.17.for_outer.near.for_inner, bf16[128,1536]{1,0:T(8,128)(2,1)S(1)} %collective-permute-done.16.for_inner.far, ...), custom_call_target="tpu_custom_call" | custom-call | flops 1811939328 | bytes 14999844 | tf_op jit(solution)/shard_map/expert_sum/pallas_call | solution.py:330
  82.2 7.5 %collective-permute-start.21 = (bf16[128,1536]{1,0:T(8,128)(2,1)S(1)}, bf16[128,1536]{1,0:T(8,128)(2,1)S(1)}, u32[]{:S(2)}, u32[]{:S(2)}) collective-permute-start(bf16[128,1536]{1,0:T(8,128)(2,1)S(1)} %payload.21.refs_0_), channel_id=1, source_target_pairs={{0,2},{1,3},{2,0},{3,1},{4,6},{5,7},{6,4},{7,5},{8,10},{9,11},{10,... | collective-permute-start | bytes 1179656 | tf_op jit(solution)/shard_map/ppermute | solution.py:395
  90.5 2.7 %expert_sum.9.refs_0_.for_outer.other = bf16[128,1536]{1,0:T(8,128)(2,1)S(1)} custom-call(s32[73]{0:T(128)S(1)} %get-tuple-element.27.refs_0_.numbers, bf16[128,1536]{1,0:T(8,128)(2,1)S(1)} %collective-permute-done.18.near.one, bf16[128,1536]{1,0:T(8,128)(2,1)S(1)} %collective-permute-done.19.far.for_inner, f32[4,256,8]{2,1,0:T(8,128)S(1)} %get-tuple-element.44.named, ...), custom_call_target="tpu_custom_call" | custom-call | flops 1811939328 | bytes 14999844 | tf_op jit(solution)/shard_map/expert_sum/pallas_call | solution.py:330
  93.2 4.2 %collective-permute-done.21.one.near = bf16[128,1536]{1,0:T(8,128)(2,1)S(1)} collective-permute-done((bf16[128,1536]{1,0:T(8,128)(2,1)S(1)}, bf16[128,1536]{1,0:T(8,128)(2,1)S(1)}, u32[]{:S(2)}, u32[]{:S(2)}) %collective-permute-start.21) | collective-permute-done | bytes 393248 | tf_op jit(solution)/shard_map/ppermute | solution.py:395
  98.5 3.9 %collective-permute-start.22 = (bf16[128,1536]{1,0:T(8,128)(2,1)S(1)}, bf16[128,1536]{1,0:T(8,128)(2,1)S(1)}, u32[]{:S(2)}, u32[]{:S(2)}) collective-permute-start(bf16[128,1536]{1,0:T(8,128)(2,1)S(1)} %payload.24), channel_id=1, source_target_pairs={{0,2},{1,3},{2,0},{3,1},{4,6},{5,7},{6,4},{7,5},{8,10},{9,11},{10,... | collective-permute-start | bytes 1179656 | tf_op jit(solution)/shard_map/ppermute | solution.py:395
  102.3 2.7 %expert_sum.11.other.refs_0_ = bf16[128,1536]{1,0:T(8,128)(2,1)S(1)} custom-call(s32[73]{0:T(128)S(1)} %get-tuple-element.27.refs_0_.numbers, bf16[128,1536]{1,0:T(8,128)(2,1)S(1)} %collective-permute-done.21.one.near, bf16[128,1536]{1,0:T(8,128)(2,1)S(1)} %collective-permute-done.13.for_outer.for_inner.near.far, f32[4,256,8]{2,1,0:T(8,128)S(1)} %get-tuple-element.44.named, ...), custom_call_target="tpu_custom_call" | custom-call | flops 1811939328 | bytes 14999844 | tf_op jit(solution)/shard_map/expert_sum/pallas_call | solution.py:330
  105.1 4.6 %collective-permute-start.25 = (bf16[128,1536]{1,0:T(8,128)(2,1)S(1)}, bf16[128,1536]{1,0:T(8,128)(2,1)S(1)}, u32[]{:S(2)}, u32[]{:S(2)}) collective-permute-start(bf16[128,1536]{1,0:T(8,128)(2,1)S(1)} %payload.25.refs_0_), channel_id=1, source_target_pairs={{0,2},{1,3},{2,0},{3,1},{4,6},{5,7},{6,4},{7,5},{8,10},{9,11},{10,... | collective-permute-start | bytes 1179656 | tf_op jit(solution)/shard_map/ppermute | solution.py:395
  112.2 2.7 %expert_sum.12.refs_0_.other = bf16[128,1536]{1,0:T(8,128)(2,1)S(1)} custom-call(s32[73]{0:T(128)S(1)} %get-tuple-element.27.refs_0_.numbers, bf16[128,1536]{1,0:T(8,128)(2,1)S(1)} %collective-permute-done.22.one.near, bf16[128,1536]{1,0:T(8,128)(2,1)S(1)} %collective-permute-done.14.near.for_outer.for_inner.far, f32[4,256,8]{2,1,0:T(8,128)S(1)} %get-tuple-element.44.named, ...), custom_call_target="tpu_custom_call" | custom-call | flops 1811939328 | bytes 14999844 | tf_op jit(solution)/shard_map/expert_sum/pallas_call | solution.py:330
  114.9 2.9 %collective-permute-done.25.one.for_outer = bf16[128,1536]{1,0:T(8,128)(2,1)S(1)} collective-permute-done((bf16[128,1536]{1,0:T(8,128)(2,1)S(1)}, bf16[128,1536]{1,0:T(8,128)(2,1)S(1)}, u32[]{:S(2)}, u32[]{:S(2)}) %collective-permute-start.25) | collective-permute-done | bytes 393248 | tf_op jit(solution)/shard_map/ppermute | solution.py:395
  118.6 5.5 %collective-permute-start.26 = (bf16[128,1536]{1,0:T(8,128)(2,1)S(1)}, bf16[128,1536]{1,0:T(8,128)(2,1)S(1)}, u32[]{:S(2)}, u32[]{:S(2)}) collective-permute-start(bf16[128,1536]{1,0:T(8,128)(2,1)S(1)} %payload.28.refs_4_), channel_id=1, source_target_pairs={{0,2},{1,3},{2,0},{3,1},{4,6},{5,7},{6,4},{7,5},{8,10},{9,11},{10,... | collective-permute-start | bytes 1179656 | tf_op jit(solution)/shard_map/ppermute | solution.py:395
  124.3 4.6 %expert_sum.13 = f32[256,1536]{1,0:T(8,128)S(1)} custom-call(s32[73]{0:T(128)S(1)} %get-tuple-element.27.refs_0_.numbers, bf16[128,1536]{1,0:T(8,128)(2,1)S(1)} %get-tuple-element.42.near, bf16[128,1536]{1,0:T(8,128)(2,1)S(1)} %get-tuple-element.43.refs_0_.for_outer.for_inner.far, f32[4,256,8]{2,1,0:T(8,128)S(1)} %get-tuple-element.44.named, ...), custom_call_target="tpu_custom_call" | custom-call | flops 3623878656 | bytes 15393060 | tf_op jit(solution)/shard_map/expert_sum/pallas_call | solution.py:330
  (94 shorter events, 26.5 us)
Async XLA Ops:
  0.0 32.6 %collective-permute-start.3 = (bf16[1,1536,1536]{2,1,0:T(8,128)(2,1)}, bf16[1,1536,1536]{2,1,0:T(8,128)(2,1)}, u32[]{:S(2)}, u32[]{:S(2)}) collective-permute-start(bf16[1,1536,1536]{2,1,0:T(8,128)(2,1)} %param.36), channel_id=1, source_target_pairs={{0,1},{1,0},{2,3},{3,2},{4,5},{5,4},{6,7},{7,6},{8,9},{9,8},{10,11... | collective-permute-start | bytes 14155784 | tf_op jit(solution)/shard_map/ppermute | solution.py:395
  0.5 32.1 %collective-permute-start.4 = (bf16[1,768,1536]{2,1,0:T(8,128)(2,1)}, bf16[1,768,1536]{2,1,0:T(8,128)(2,1)S(1)}, u32[]{:S(2)}, u32[]{:S(2)}) collective-permute-start(bf16[1,768,1536]{2,1,0:T(8,128)(2,1)} %param.37), channel_id=1, source_target_pairs={{0,1},{1,0},{2,3},{3,2},{4,5},{5,4},{6,7},{7,6},{8,9},{9,8},{10,11... | collective-permute-start | bytes 7077896 | tf_op jit(solution)/shard_map/ppermute | solution.py:395
  2.1 12.1 %collective-permute-start.2 = (bf16[5,16,512]{2,1,0:T(8,128)(2,1)S(1)}, bf16[5,16,512]{2,1,0:T(8,128)(2,1)S(1)}, u32[]{:S(2)}, u32[]{:S(2)}) collective-permute-start(bf16[5,16,512]{2,1,0:T(8,128)(2,1)S(1)} %pad_maximum_fusion.1.refs_7_), channel_id=1, source_target_pairs={{0,6},{1,7},{2,4},{3,5},{4,2},{5,3},{6,0},{7,1},{8,14},{9,15},{10,... | collective-permute-start | bytes 245768 | tf_op jit(solution)/shard_map/ppermute | solution.py:395
  7.2 7.1 %collective-permute-start.1 = (bf16[5,16,512]{2,1,0:T(8,128)(2,1)S(1)}, bf16[5,16,512]{2,1,0:T(8,128)(2,1)S(1)}, u32[]{:S(2)}, u32[]{:S(2)}) collective-permute-start(bf16[5,16,512]{2,1,0:T(8,128)(2,1)S(1)} %pad_maximum_fusion.1.refs_7_), channel_id=1, source_target_pairs={{0,4},{1,5},{2,6},{3,7},{4,0},{5,1},{6,2},{7,3},{8,12},{9,13},{10,... | collective-permute-start | bytes 245768 | tf_op jit(solution)/shard_map/ppermute | solution.py:395
  7.2 7.1 %collective-permute-start = (bf16[5,16,512]{2,1,0:T(8,128)(2,1)S(1)}, bf16[5,16,512]{2,1,0:T(8,128)(2,1)S(1)}, u32[]{:S(2)}, u32[]{:S(2)}) collective-permute-start(bf16[5,16,512]{2,1,0:T(8,128)(2,1)S(1)} %pad_maximum_fusion.1.refs_7_), channel_id=1, source_target_pairs={{0,2},{1,3},{2,0},{3,1},{4,6},{5,7},{6,4},{7,5},{8,10},{9,11},{10,... | collective-permute-start | bytes 245768 | tf_op jit(solution)/shard_map/ppermute | solution.py:395
  15.2 11.0 %collective-permute-start.7 = (bf16[16,16,512]{2,1,0:T(8,128)(2,1)S(1)}, bf16[16,16,512]{2,1,0:T(8,128)(2,1)S(1)}, u32[]{:S(2)}, u32[]{:S(2)}) collective-permute-start(bf16[16,16,512]{2,1,0:T(8,128)(2,1)S(1)} %after.2.refs_0_), channel_id=1, source_target_pairs={{0,24},{8,16},{16,8},{24,0},{1,25},{9,17},{17,9},{25,1},{2,26},{10... | collective-permute-start | bytes 786440 | tf_op jit(solution)/shard_map/ppermute | solution.py:395
  17.8 11.6 %collective-permute-start.6 = (bf16[16,16,512]{2,1,0:T(8,128)(2,1)S(1)}, bf16[16,16,512]{2,1,0:T(8,128)(2,1)S(1)}, u32[]{:S(2)}, u32[]{:S(2)}) collective-permute-start(bf16[16,16,512]{2,1,0:T(8,128)(2,1)S(1)} %after.2.refs_0_), channel_id=1, source_target_pairs={{0,16},{8,24},{16,0},{24,8},{1,17},{9,25},{17,1},{25,9},{2,18},{10... | collective-permute-start | bytes 786440 | tf_op jit(solution)/shard_map/ppermute | solution.py:395
  18.3 11.2 %collective-permute-start.5 = (bf16[16,16,512]{2,1,0:T(8,128)(2,1)S(1)}, bf16[16,16,512]{2,1,0:T(8,128)(2,1)S(1)}, u32[]{:S(2)}, u32[]{:S(2)}) collective-permute-start(bf16[16,16,512]{2,1,0:T(8,128)(2,1)S(1)} %after.2.refs_0_), channel_id=1, source_target_pairs={{0,8},{8,0},{16,24},{24,16},{1,9},{9,1},{17,25},{25,17},{2,10},{10... | collective-permute-start | bytes 786440 | tf_op jit(solution)/shard_map/ppermute | solution.py:395
  38.9 12.3 %collective-permute-start.13 = (bf16[128,1536]{1,0:T(8,128)(2,1)S(1)}, bf16[128,1536]{1,0:T(8,128)(2,1)S(1)}, u32[]{:S(2)}, u32[]{:S(2)}) collective-permute-start(bf16[128,1536]{1,0:T(8,128)(2,1)S(1)} %get-tuple-element.42.near), channel_id=1, source_target_pairs={{0,2},{1,3},{2,0},{3,1},{4,6},{5,7},{6,4},{7,5},{8,10},{9,11},{10,... | collective-permute-start | bytes 1179656 | tf_op jit(solution)/shard_map/ppermute | solution.py:395
  41.5 10.5 %collective-permute-start.12 = (bf16[128,1536]{1,0:T(8,128)(2,1)S(1)}, bf16[128,1536]{1,0:T(8,128)(2,1)S(1)}, u32[]{:S(2)}, u32[]{:S(2)}) collective-permute-start(bf16[128,1536]{1,0:T(8,128)(2,1)S(1)} %get-tuple-element.42.near), channel_id=1, source_target_pairs={{2,4},{3,5},{4,2},{5,3},{10,12},{11,13},{12,10},{13,11},{18,20},{1... | collective-permute-start | bytes 1179656 | tf_op jit(solution)/shard_map/ppermute | solution.py:483
  51.3 7.6 %collective-permute-start.15 = (bf16[128,1536]{1,0:T(8,128)(2,1)S(1)}, bf16[128,1536]{1,0:T(8,128)(2,1)S(1)}, u32[]{:S(2)}, u32[]{:S(2)}) collective-permute-start(bf16[128,1536]{1,0:T(8,128)(2,1)S(1)} %payload.15.refs_0_), channel_id=1, source_target_pairs={{2,4},{3,5},{4,2},{5,3},{10,12},{11,13},{12,10},{13,11},{18,20},{1... | collective-permute-start | bytes 1179656 | tf_op jit(solution)/shard_map/ppermute | solution.py:479
  52.1 14.1 %collective-permute-start.14 = (bf16[128,1536]{1,0:T(8,128)(2,1)S(1)}, bf16[128,1536]{1,0:T(8,128)(2,1)S(1)}, u32[]{:S(2)}, u32[]{:S(2)}) collective-permute-start(bf16[128,1536]{1,0:T(8,128)(2,1)S(1)} %payload.16), channel_id=1, source_target_pairs={{0,2},{1,3},{2,0},{3,1},{4,6},{5,7},{6,4},{7,5},{8,10},{9,11},{10,... | collective-permute-start | bytes 1179656 | tf_op jit(solution)/shard_map/ppermute | solution.py:395
  59.0 16.6 %collective-permute-start.17 = (bf16[128,1536]{1,0:T(8,128)(2,1)S(1)}, bf16[128,1536]{1,0:T(8,128)(2,1)S(1)}, u32[]{:S(2)}, u32[]{:S(2)}) collective-permute-start(bf16[128,1536]{1,0:T(8,128)(2,1)S(1)} %payload.17.refs_0_), channel_id=1, source_target_pairs={{0,2},{1,3},{2,0},{3,1},{4,6},{5,7},{6,4},{7,5},{8,10},{9,11},{10,... | collective-permute-start | bytes 1179656 | tf_op jit(solution)/shard_map/ppermute | solution.py:395
  66.3 10.1 %collective-permute-start.16 = (bf16[128,1536]{1,0:T(8,128)(2,1)S(1)}, bf16[128,1536]{1,0:T(8,128)(2,1)S(1)}, u32[]{:S(2)}, u32[]{:S(2)}) collective-permute-start(bf16[128,1536]{1,0:T(8,128)(2,1)S(1)} %payload.18), channel_id=1, source_target_pairs={{2,4},{3,5},{4,2},{5,3},{10,12},{11,13},{12,10},{13,11},{18,20},{1... | collective-permute-start | bytes 1179656 | tf_op jit(solution)/shard_map/ppermute | solution.py:479
  75.7 6.5 %collective-permute-start.19 = (bf16[128,1536]{1,0:T(8,128)(2,1)S(1)}, bf16[128,1536]{1,0:T(8,128)(2,1)S(1)}, u32[]{:S(2)}, u32[]{:S(2)}) collective-permute-start(bf16[128,1536]{1,0:T(8,128)(2,1)S(1)} %payload.19.refs_0_), channel_id=1, source_target_pairs={{2,4},{3,5},{4,2},{5,3},{10,12},{11,13},{12,10},{13,11},{18,20},{1... | collective-permute-start | bytes 1179656 | tf_op jit(solution)/shard_map/ppermute | solution.py:479
  76.5 13.3 %collective-permute-start.18 = (bf16[128,1536]{1,0:T(8,128)(2,1)S(1)}, bf16[128,1536]{1,0:T(8,128)(2,1)S(1)}, u32[]{:S(2)}, u32[]{:S(2)}) collective-permute-start(bf16[128,1536]{1,0:T(8,128)(2,1)S(1)} %payload.20), channel_id=1, source_target_pairs={{0,2},{1,3},{2,0},{3,1},{4,6},{5,7},{6,4},{7,5},{8,10},{9,11},{10,... | collective-permute-start | bytes 1179656 | tf_op jit(solution)/shard_map/ppermute | solution.py:395
  82.2 15.1 %collective-permute-start.21 = (bf16[128,1536]{1,0:T(8,128)(2,1)S(1)}, bf16[128,1536]{1,0:T(8,128)(2,1)S(1)}, u32[]{:S(2)}, u32[]{:S(2)}) collective-permute-start(bf16[128,1536]{1,0:T(8,128)(2,1)S(1)} %payload.21.refs_0_), channel_id=1, source_target_pairs={{0,2},{1,3},{2,0},{3,1},{4,6},{5,7},{6,4},{7,5},{8,10},{9,11},{10,... | collective-permute-start | bytes 1179656 | tf_op jit(solution)/shard_map/ppermute | solution.py:395
  89.8 8.5 %collective-permute-start.20 = (bf16[128,1536]{1,0:T(8,128)(2,1)S(1)}, bf16[128,1536]{1,0:T(8,128)(2,1)S(1)}, u32[]{:S(2)}, u32[]{:S(2)}) collective-permute-start(bf16[128,1536]{1,0:T(8,128)(2,1)S(1)} %payload.22), channel_id=1, source_target_pairs={{2,4},{3,5},{4,2},{5,3},{10,12},{11,13},{12,10},{13,11},{18,20},{1... | collective-permute-start | bytes 1179656 | tf_op jit(solution)/shard_map/ppermute | solution.py:479
  97.5 7.5 %collective-permute-start.23 = (bf16[128,1536]{1,0:T(8,128)(2,1)S(1)}, bf16[128,1536]{1,0:T(8,128)(2,1)S(1)}, u32[]{:S(2)}, u32[]{:S(2)}) collective-permute-start(bf16[128,1536]{1,0:T(8,128)(2,1)S(1)} %payload.23.refs_1_), channel_id=1, source_target_pairs={{2,4},{3,5},{4,2},{5,3},{10,12},{11,13},{12,10},{13,11},{18,20},{1... | collective-permute-start | bytes 1179656 | tf_op jit(solution)/shard_map/ppermute | solution.py:479
  98.5 12.9 %collective-permute-start.22 = (bf16[128,1536]{1,0:T(8,128)(2,1)S(1)}, bf16[128,1536]{1,0:T(8,128)(2,1)S(1)}, u32[]{:S(2)}, u32[]{:S(2)}) collective-permute-start(bf16[128,1536]{1,0:T(8,128)(2,1)S(1)} %payload.24), channel_id=1, source_target_pairs={{0,2},{1,3},{2,0},{3,1},{4,6},{5,7},{6,4},{7,5},{8,10},{9,11},{10,... | collective-permute-start | bytes 1179656 | tf_op jit(solution)/shard_map/ppermute | solution.py:395
  105.1 12.6 %collective-permute-start.25 = (bf16[128,1536]{1,0:T(8,128)(2,1)S(1)}, bf16[128,1536]{1,0:T(8,128)(2,1)S(1)}, u32[]{:S(2)}, u32[]{:S(2)}) collective-permute-start(bf16[128,1536]{1,0:T(8,128)(2,1)S(1)} %payload.25.refs_0_), channel_id=1, source_target_pairs={{0,2},{1,3},{2,0},{3,1},{4,6},{5,7},{6,4},{7,5},{8,10},{9,11},{10,... | collective-permute-start | bytes 1179656 | tf_op jit(solution)/shard_map/ppermute | solution.py:395
  111.5 7.0 %collective-permute-start.24 = (bf16[128,1536]{1,0:T(8,128)(2,1)S(1)}, bf16[128,1536]{1,0:T(8,128)(2,1)S(1)}, u32[]{:S(2)}, u32[]{:S(2)}) collective-permute-start(bf16[128,1536]{1,0:T(8,128)(2,1)S(1)} %payload.26), channel_id=1, source_target_pairs={{2,4},{3,5},{4,2},{5,3},{10,12},{11,13},{12,10},{13,11},{18,20},{1... | collective-permute-start | bytes 1179656 | tf_op jit(solution)/shard_map/ppermute | solution.py:479
  117.8 11.0 %collective-permute-start.27 = (bf16[128,1536]{1,0:T(8,128)(2,1)S(1)}, bf16[128,1536]{1,0:T(8,128)(2,1)S(1)}, u32[]{:S(2)}, u32[]{:S(2)}) collective-permute-start(bf16[128,1536]{1,0:T(8,128)(2,1)S(1)} %payload.27.refs_0_), channel_id=1, source_target_pairs={{2,4},{3,5},{4,2},{5,3},{10,12},{11,13},{12,10},{13,11},{18,20},{1... | collective-permute-start | bytes 1179656 | tf_op jit(solution)/shard_map/ppermute | solution.py:479
  118.6 11.2 %collective-permute-start.26 = (bf16[128,1536]{1,0:T(8,128)(2,1)S(1)}, bf16[128,1536]{1,0:T(8,128)(2,1)S(1)}, u32[]{:S(2)}, u32[]{:S(2)}) collective-permute-start(bf16[128,1536]{1,0:T(8,128)(2,1)S(1)} %payload.28.refs_4_), channel_id=1, source_target_pairs={{0,2},{1,3},{2,0},{3,1},{4,6},{5,7},{6,4},{7,5},{8,10},{9,11},{10,... | collective-permute-start | bytes 1179656 | tf_op jit(solution)/shard_map/ppermute | solution.py:395
  (15 other events, 95.1 us)

commit v2 on v1

--- a/solution.py
+++ b/solution.py
@@ -65,11 +65,11 @@
 
     def place(index, carry):
         page = page_table[prompts[index // PPP] * PPP + index % PPP]
-        owner = page // pages_each
-        apart = (owner % exp_size) ^ exp
-        apart_req = (owner // exp_size) ^ req
-        block = ((apart % 2) * req_size + apart_req) * (exp_size // 2) + apart // 2
-        numbers[1 + 2 * requests + index] = block * pages_each + page % pages_each
+        owner = lax.div(page, pages_each)
+        apart = lax.rem(owner, exp_size) ^ exp
+        apart_req = lax.div(owner, exp_size) ^ req
+        block = ((apart & 1) * req_size + apart_req) * (exp_size // 2) + (apart >> 1)
+        numbers[1 + 2 * requests + index] = block * pages_each + lax.rem(page, pages_each)
         return carry
 
     lax.fori_loop(0, requests * PPP, place, 0)
@@ -181,15 +181,17 @@
     got_tokens = copies([(tokens.at[pl.ds(0, rows)], token_rows)], token_semaphore)
     got = copies(list(zip(there, held)), semaphores)
     scalars = Scalars(numbers, requests)
-    for copy in got_parts:
-        copy.wait()
 
     def fetch(index, carry):
         prompt_rows[index] = cache[scalars.place(index)]
         return carry
 
-    lax.fori_loop(0, requests * PPP, fetch, 0, unroll=4)
-    attend(0, rows, scalars, query_rows, keys, values, prompt_rows, attended)
+    def fetch_pages():
+        for copy in got_parts:
+            copy.wait()
+        lax.fori_loop(0, requests * PPP, fetch, 0, unroll=4)
+
+    attend(0, rows, scalars, query_rows, keys, values, prompt_rows, attended, fetch_pages)
     for copy in got_tokens + got[:3]:
         copy.wait()
     project(0, scalars, gain, attended, token_rows, held[:3], hidden, normed, scratch)
@@ -208,11 +210,14 @@
     project(first_row, scalars, gain, attended, token_rows, weights, hidden, normed, scratch)
 
 
-def attend(first_row, count, scalars, query_rows, keys, values, prompt_rows, attended):
+def attend(
+    first_row, count, scalars, query_rows, keys, values, prompt_rows, attended, then=lambda: None
+):
     starts = scalars.starts
     requests = len(starts)
     group = QUERY_HEADS // KEY_VALUE_HEADS
     factor = HEAD_WIDTH ** (-0.5) * LOG2_E
+    tiles = []
     for begin in range(first_row, first_row + count, TILE):
         end = begin + TILE
         window = max(0, begin - SEGMOST)
@@ -239,8 +244,11 @@
             state.append(
                 (largest, total, dot(weights.astype(jnp.bfloat16), values[window:end, lanes[head]]))
             )
-
-        def add_prompt(slot, state):
+        tiles.append((begin, end, row_slot, grouped, state))
+    then()
+    for begin, end, row_slot, grouped, state in tiles:
+
+        def add_prompt(slot, state, row_slot=row_slot, grouped=grouped):
             prompt_pages = prompt_rows[pl.ds(slot * PPP, PPP)]
             prompt = prompt_pages.reshape(PROMPT_LENGTH, prompt_pages.shape[-1])
             apart = jnp.where(row_slot == slot, 0.0, VERY_NEGATIVE)
@@ -290,16 +298,7 @@
     normed[...] = (scratch[...] * scale * wide).astype(jnp.bfloat16)
 
 
-def expert_kernel(plan, numbers, near, far, named, router, *refs):
-    weights, (out, units) = refs[:4], refs[-2:]
-    exp = numbers[0]
-    chip = exp // 2
-    use_near, owner, start = plan(chip)
-    if use_near is None:
-        rows = jnp.concatenate([near[...], far[...]], axis=0)
-    else:
-        rows = jnp.where(use_near, near[...], far[...])
-    mentioned = named[chip ^ owner, pl.ds(start, rows.shape[0]), :]
+def gated_experts(exp, rows, mentioned, router, weights, units):
     squashed = jnp.where(mentioned > 0.0, jax.nn.sigmoid(dot_transposed(rows, router[...])), 0.0)
     gates = squashed / jnp.sum(squashed, axis=1, keepdims=True)
     lane = lax.broadcasted_iota(jnp.int32, gates.shape, 1)
@@ -322,7 +321,31 @@
         for number in range(2):
             result = dot(units[number], weights[2 * number + 1][:, columns]).astype(jnp.bfloat16)
             total = total + gate_columns[number] * result.astype(jnp.float32)
+        yield columns, total
+
+
+def expert_kernel(plan, numbers, near, far, named, router, *refs):
+    weights, (out, units) = refs[:4], refs[4:]
+    exp = numbers[0]
+    chip = exp // 2
+    use_near, owner, start = plan(chip)
+    rows = jnp.where(use_near, near[...], far[...])
+    mentioned = named[chip ^ owner, pl.ds(start, rows.shape[0]), :]
+    for columns, total in gated_experts(exp, rows, mentioned, router, weights, units):
         out[:, columns] = total.astype(out.dtype)
+
+
+def own_kernel(numbers, first, second, named, router, *refs):
+    weights, refs = refs[:4], refs[4:]
+    hidden_first, hidden_second, back, other_back = refs[:4]
+    out_first, out_second, units = refs[-3:]
+    rows = jnp.concatenate([first[...], second[...]], axis=0)
+    half = first.shape[0]
+    for columns, total in gated_experts(numbers[0], rows, named[0], router, weights, units):
+        came = back[:, columns].astype(jnp.float32) + other_back[:, columns].astype(jnp.float32)
+        upper = hidden_first[:, columns].astype(jnp.float32) + total[:half] + came
+        out_first[:, columns] = upper.astype(jnp.bfloat16)
+        out_second[:, columns] = hidden_second[:, columns].astype(jnp.float32) + total[half:]
 
 
 def call(kernel, inputs, specs, outs, scratch, name, flops, limit, out_specs=None):
@@ -339,20 +362,39 @@
     )(*inputs)
 
 
-def expert_sum(near, far, plan, shared, dtype, rows=None, earlier=()):
+def expert_sum(near, far, plan, shared, dtype):
     numbers, named, router, weights = shared
-    rows = near.shape[0] if rows is None else rows
+    rows = near.shape[0]
     hidden_units, width = weights[1].shape
     return call(
         functools.partial(expert_kernel, plan),
-        [numbers, near, far, named, router, *weights, *earlier],
-        [SMEM] + [VMEM] * 8 + [ANY] * len(earlier),
+        [numbers, near, far, named, router, *weights],
+        [SMEM] + [VMEM] * 8,
         [jax.ShapeDtypeStruct((rows, width), dtype)],
         [pltpu.VMEM((2, rows, hidden_units), jnp.bfloat16)],
         "expert_sum",
         12 * rows * width * hidden_units,
         10,
     )[0]
+
+
+def own_sum(halves, hidden, back, other_back, shared, *earlier):
+    numbers, named, router, weights = shared
+    half, width = halves[0].shape
+    hidden_units = weights[1].shape[0]
+    return call(
+        own_kernel,
+        [numbers, *halves, named, router, *weights, *hidden, back, other_back, *earlier],
+        [SMEM] + [VMEM] * 12 + [ANY] * len(earlier),
+        [
+            jax.ShapeDtypeStruct((half, width), jnp.bfloat16),
+            jax.ShapeDtypeStruct((half, width), jnp.float32),
+        ],
+        [pltpu.VMEM((2, 2 * half, hidden_units), jnp.bfloat16)],
+        "own_sum",
+        24 * half * width * hidden_units,
+        12,
+    )
 
 
 def after(values, *earlier):
@@ -374,6 +416,11 @@
 def added_kernel(one, other, *refs):
     total = one[...].astype(jnp.float32) + other[...].astype(jnp.float32)
     refs[-1][...] = total.astype(jnp.bfloat16)
+
+
+def added_inside_kernel(outer, one, other, *refs):
+    total = one[...].astype(jnp.float32) + other[...].astype(jnp.float32)
+    refs[-1][...] = jnp.where(outer[0:1, 0:1] > 0.0, 0.0, total).astype(jnp.bfloat16)
 
 
 def payload(kernel, inputs, earlier):
@@ -409,7 +456,7 @@
     return lax.ppermute(values, "exp", [(i, (i + 2) % size) for i in range(size)])
 
 
-def ring_experts(halves, shared, outer_here):
+def ring_experts(halves, hidden, shared, outer_here):
     chips = lax.axis_size("exp") // 2
     own = jnp.concatenate(halves, axis=0)
     rows, partial = own, None
@@ -423,7 +470,8 @@
     total = expert_sum(own, own, lambda chip: (True, chip, 0), shared, jnp.float32)
     if partial is not None:
         total = total + next_chip(partial).astype(jnp.float32)
-    return total
+    total = total + jnp.concatenate(hidden, axis=0).astype(jnp.float32)
+    return total.astype(jnp.bfloat16)
 
 
 COMPUTED = {
@@ -443,11 +491,11 @@
     return found
 
 
-def line_experts(halves, shared, outer_here):
+def line_experts(halves, hidden, shared, outer_here):
     size = lax.axis_size("exp")
     first, second = halves
     half = first.shape[0]
-    inner_pairs = [(i, i ^ 6) for i in range(2, size - 2)]
+    middle_pairs = [(i, i ^ (6 if 2 <= i < size - 2 else 1)) for i in range(size)]
 
     def chosen(for_outer, for_inner, *earlier):
         return payload(chosen_kernel, [outer_here, for_outer, for_inner], earlier)
@@ -475,12 +523,13 @@
         elif slot == 4:
             rows = chosen(side[3], second, *earlier)
         else:
-            rows = added(side[slot - 1], sums[slot - 3], *earlier)
-        middle[slot] = lax.ppermute(rows, "exp", inner_pairs)
+            inputs = [outer_here, side[slot - 1], sums[slot - 3]]
+            rows = payload(added_inside_kernel, inputs, earlier)
+        middle[slot] = lax.ppermute(rows, "exp", middle_pairs)
         return rows
 
     side[1] = swap(first, "exp", 2)
-    middle[1] = lax.ppermute(first, "exp", inner_pairs)
+    middle[1] = lax.ppermute(first, "exp", middle_pairs)
     last = second
     for slot in range(2, 9):
         if slot % 2:
@@ -498,11 +547,10 @@
 
             sums[slot] = expert_sum(side[slot - 1], inner_rows, plan, shared, jnp.bfloat16)
             last = sums[slot]
-    plan = lambda chip: (None, chip, 0)
-    total = expert_sum(first, second, plan, shared, jnp.float32, 2 * half, (sent,))
-    back = chosen(side[7], side[3]).astype(jnp.float32) + middle[5].astype(jnp.float32)
-    back_second = side[8].astype(jnp.float32) + middle[8].astype(jnp.float32)
-    return total + jnp.concatenate([back, back_second], axis=0)
+    back = chosen(side[7], side[3])
+    upper, lower = own_sum(halves, hidden, back, middle[5], shared, sent)
+    lower = lower + side[8].astype(jnp.float32) + middle[8].astype(jnp.float32)
+    return jnp.concatenate([upper, lower.astype(jnp.bfloat16)], axis=0)
 
 
 def on_device(
@@ -625,12 +673,9 @@
         2 * count * width * width,
         8,
     )
-    hidden_state = jnp.concatenate([hidden_first, hidden_second], axis=0)
-    halves, weights = (first, second), held[3:]
+    shared = (numbers, named, router.T, held[3:])
     experts_of = line_experts if lax.axis_size("exp") == 8 else ring_experts
-    shared = (numbers, named, router.T, weights)
-    mixed_rows = hidden_state.astype(jnp.float32) + experts_of(halves, shared, outer_here)
-    return mixed_rows.astype(jnp.bfloat16)
+    return experts_of((first, second), (hidden_first, hidden_second), shared, outer_here)
 
 
 def solution(mesh):

time: 131 us -> 124 us (0.947)
  starting transfers between devices: 54.5 us -> 38.6 us
  waiting for transfers between devices: 23.7 us -> 32.6 us
    ppermute x20, starting transfers between devices: 48.8 us -> 38.1 us  [swap(): return lax.ppermute(values, axis, [(i, i ^ distance) for i in range(size)])]
    ppermute x20, waiting for transfers between devices: 23.7 us -> 32.6 us  [swap(): return lax.ppermute(values, axis, [(i, i ^ distance) for i in range(size)])]
    ppermute x8, starting transfers between devices: 5.69 us -> 0.43 us  [the longest x7 0.43 us: send_middle(): middle[slot] = lax.ppermute(rows, 'exp', middle_pairs)]
  transfers between devices with their start and end apart: 28 -> 28, of which waited for: 13 -> 14; matrix products, arithmetic and copies ran while one was open for 2% -> 2% of each run, Pallas kernels for 30% -> 31%
where the time goes in v2:
time: 124 us
  Pallas kernels  45.3 us (37%)
  starting transfers between devices  38.6 us (31%)
  waiting for transfers between devices  32.6 us (26%)
  other arithmetic  3.57 us (3%)
  local copies, waits for them, and re-layouts  3.4 us (3%)
    pallas_call x26, Pallas kernels, call(): pl.pallas_call(kernel, in_specs=specs, out_specs=out_specs or [VMEM] * le...  45.3 us
    ppermute x20, starting transfers between devices, swap(): return lax.ppermute(values, axis, [(i, i ^ distance) for i in range(size)])  38.1 us
    ppermute x20, waiting for transfers between devices, swap(): return lax.ppermute(values, axis, [(i, i ^ distance) for i in range(size)])  32.6 us
    unnamed x22, local copies, waits for them, and re-layouts  3.36 us
  transfers between devices with their start and end apart: 28, of which 14 were waited for; matrix products, arithmetic and copies ran while one was open for 2% of the time, Pallas kernels for 31%

profile of v2, /device:TPU:0, one launch (start us, length us, event | category | flops | bytes accessed | tf_op | source)
XLA Modules:
  0.0 123.9 jit_solution(5968263961563034380)
XLA Ops:
  2.1 5.1 %collective-permute-start.2 = (bf16[5,16,512]{2,1,0:T(8,128)(2,1)S(1)}, bf16[5,16,512]{2,1,0:T(8,128)(2,1)S(1)}, u32[]{:S(2)}, u32[]{:S(2)}) collective-permute-start(bf16[5,16,512]{2,1,0:T(8,128)(2,1)S(1)} %pad_maximum_fusion.2.refs_7_), channel_id=1, source_target_pairs={{0,6},{1,7},{2,4},{3,5},{4,2},{5,3},{6,0},{7,1},{8,14},{9,15},{10,... | collective-permute-start | bytes 245768 | tf_op jit(solution)/shard_map/ppermute | solution.py:442
  10.5 2.8 %prepare.1 = (s32[73]{0:T(128)S(1)}, f32[8,128]{1,0:T(8,128)S(1)}) custom-call(s32[2]{0:T(128)S(1)} %pad_add_fusion.where, s32[1,256]{1,0:T(1,128)S(1)} %copy-done.7, s32[4]{0:T(128)S(1)} %copy-done.8, s32[4]{0:T(128)S(1)} %copy-done.9, s32[128]{0:T(128)S(1)} %copy-done.10), custom_call_target="tpu_custom_call" | custom-call | flops 393216 | bytes 1576 | tf_op jit(solution)/shard_map/prepare/pallas_call | solution.py:353
  15.1 2.5 %collective-permute-start.7 = (bf16[16,16,512]{2,1,0:T(8,128)(2,1)S(1)}, bf16[16,16,512]{2,1,0:T(8,128)(2,1)S(1)}, u32[]{:S(2)}, u32[]{:S(2)}) collective-permute-start(bf16[16,16,512]{2,1,0:T(8,128)(2,1)S(1)} %after.2.refs_0_), channel_id=1, source_target_pairs={{0,24},{8,16},{16,8},{24,0},{1,25},{9,17},{17,9},{25,1},{2,26},{10... | collective-permute-start | bytes 786440 | tf_op jit(solution)/shard_map/ppermute | solution.py:442
  19.4 7.4 %projections.1 = (bf16[256,1536]{1,0:T(8,128)(2,1)S(1)}, bf16[256,256]{1,0:T(8,128)(2,1)S(1)}, bf16[256,256]{1,0:T(8,128)(2,1)S(1)}, f32[4,256,8]{2,1,0:T(8,128)S(1)}) custom-call(s32[73]{0:T(128)S(1)} %get-tuple-element.29.refs_0_.numbers, bf16[1536]{0:T(1024)(128)(2,1)S(1)} %copy-done.6, bf16[256,1536]{1,0:T(8,128)(2,1)} %refs_5_.5, ...), custom_call_target="tpu_custom_call" | custom-call | flops 1811939328 | bytes 8981796 | tf_op jit(solution)/shard_map/projections/pallas_call | solution.py:353
  26.8 2.4 %collective-permute-done.6.refs_2_ = bf16[16,16,512]{2,1,0:T(8,128)(2,1)S(1)} collective-permute-done((bf16[16,16,512]{2,1,0:T(8,128)(2,1)S(1)}, bf16[16,16,512]{2,1,0:T(8,128)(2,1)S(1)}, u32[]{:S(2)}, u32[]{:S(2)}) %collective-permute-start.6) | collective-permute-done | bytes 262176 | tf_op jit(solution)/shard_map/ppermute | solution.py:442
  32.5 6.9 %first_attention.1 = (bf16[128,1536]{1,0:T(8,128)(2,1)S(1)}, bf16[128,1536]{1,0:T(8,128)(2,1)S(1)}, bf16[64,16,512]{2,1,0:T(8,128)(2,1)S(1)}, bf16[1536,1536]{1,...) custom-call(s32[73]{0:T(128)S(1)} %get-tuple-element.29.refs_0_.numb, ...), custom_call_target="tpu_custom_call" | custom-call | flops 1207959552 | bytes 24382756 | tf_op jit(solution)/shard_map/first_attention/pallas_call | solution.py:353
  40.2 5.6 %second_attention.1 = (bf16[128,1536]{1,0:T(8,128)(2,1)S(1)}, bf16[128,1536]{1,0:T(8,128)(2,1)S(1)}) custom-call(s32[73]{0:T(128)S(1)} %get-tuple-element.29.refs_0_.numbers, bf16[1536]{0:T(1024)(128)(2,1)S(1)} %copy-done.5, bf16[256,1536]{1,0:T(8,128)(2,1)S(1)} %get-tuple-element.30.refs_2_, bf16[256,256]{1,0:T(8,128)(2,1)S(1)} %get-tuple-element.31.refs_4_.refs_3_, ...), custom_call_target="tpu_custom_call" | custom-call | flops 1207959552 | bytes 9178404 | tf_op jit(solution)/shard_map/second_attention/pallas_call | solution.py:353
  45.8 4.1 %collective-permute-done.12.near.for_outer.for_inner.far = bf16[128,1536]{1,0:T(8,128)(2,1)S(1)} collective-permute-done((bf16[128,1536]{1,0:T(8,128)(2,1)S(1)}, bf16[128,1536]{1,0:T(8,128)(2,1)S(1)}, u32[]{:S(2)}, u32[]{:S(2)}) %collective-permute-start.12) | collective-permute-done | bytes 393248 | tf_op jit(solution)/shard_map/ppermute | solution.py:442
  50.2 2.9 %collective-permute-start.16 = (bf16[128,1536]{1,0:T(8,128)(2,1)S(1)}, bf16[128,1536]{1,0:T(8,128)(2,1)S(1)}, u32[]{:S(2)}, u32[]{:S(2)}) collective-permute-start(bf16[128,1536]{1,0:T(8,128)(2,1)S(1)} %payload.17), channel_id=1, source_target_pairs={{0,2},{1,3},{2,0},{3,1},{4,6},{5,7},{6,4},{7,5},{8,10},{9,11},{10,... | collective-permute-start | bytes 1179656 | tf_op jit(solution)/shard_map/ppermute | solution.py:442
  53.1 2.6 %expert_sum.6.for_outer.refs_0_.other = bf16[128,1536]{1,0:T(8,128)(2,1)S(1)} custom-call(s32[73]{0:T(128)S(1)} %get-tuple-element.29.refs_0_.numbers, bf16[128,1536]{1,0:T(8,128)(2,1)S(1)} %collective-permute-done.12.near.for_outer.for_inner.far, bf16[128,1536]{1,0:T(8,128)(2,1)S(1)} %collective-permute-done.13.far.for_inner, ...), custom_call_target="tpu_custom_call" | custom-call | flops 1811939328 | bytes 14999844 | tf_op jit(solution)/shard_map/expert_sum/pallas_call | solution.py:353
  55.8 6.5 %collective-permute-start.15 = (bf16[128,1536]{1,0:T(8,128)(2,1)S(1)}, bf16[128,1536]{1,0:T(8,128)(2,1)S(1)}, u32[]{:S(2)}, u32[]{:S(2)}) collective-permute-start(bf16[128,1536]{1,0:T(8,128)(2,1)S(1)} %payload.16.refs_0_), channel_id=1, source_target_pairs={{0,2},{1,3},{2,0},{3,1},{4,6},{5,7},{6,4},{7,5},{8,10},{9,11},{10,... | collective-permute-start | bytes 1179656 | tf_op jit(solution)/shard_map/ppermute | solution.py:442
  62.5 2.7 %expert_sum.8.refs_0_.for_outer.other = bf16[128,1536]{1,0:T(8,128)(2,1)S(1)} custom-call(s32[73]{0:T(128)S(1)} %get-tuple-element.29.refs_0_.numbers, bf16[128,1536]{1,0:T(8,128)(2,1)S(1)} %collective-permute-done.16.for_outer.for_inner.near.far, bf16[128,1536]{1,0:T(8,128)(2,1)S(1)} %collective-permute-done.14.for_inner.far, ...), custom_call_target="tpu_custom_call" | custom-call | flops 1811939328 | bytes 14999844 | tf_op jit(solution)/shard_map/expert_sum/pallas_call | solution.py:353
  65.1 5.9 %collective-permute-done.15.near.for_outer.for_inner = bf16[128,1536]{1,0:T(8,128)(2,1)S(1)} collective-permute-done((bf16[128,1536]{1,0:T(8,128)(2,1)S(1)}, bf16[128,1536]{1,0:T(8,128)(2,1)S(1)}, u32[]{:S(2)}, u32[]{:S(2)}) %collective-permute-start.15) | collective-permute-done | bytes 393248 | tf_op jit(solution)/shard_map/ppermute | solution.py:442
  71.3 3.2 %collective-permute-start.20 = (bf16[128,1536]{1,0:T(8,128)(2,1)S(1)}, bf16[128,1536]{1,0:T(8,128)(2,1)S(1)}, u32[]{:S(2)}, u32[]{:S(2)}) collective-permute-start(bf16[128,1536]{1,0:T(8,128)(2,1)S(1)} %payload.21), channel_id=1, source_target_pairs={{0,2},{1,3},{2,0},{3,1},{4,6},{5,7},{6,4},{7,5},{8,10},{9,11},{10,... | collective-permute-start | bytes 1179656 | tf_op jit(solution)/shard_map/ppermute | solution.py:442
  74.5 2.6 %expert_sum.7.for_outer.refs_0_.other = bf16[128,1536]{1,0:T(8,128)(2,1)S(1)} custom-call(s32[73]{0:T(128)S(1)} %get-tuple-element.29.refs_0_.numbers, bf16[128,1536]{1,0:T(8,128)(2,1)S(1)} %collective-permute-done.15.near.for_outer.for_inner, bf16[128,1536]{1,0:T(8,128)(2,1)S(1)} %collective-permute-done.17.far.for_inner, ...), custom_call_target="tpu_custom_call" | custom-call | flops 1811939328 | bytes 14999844 | tf_op jit(solution)/shard_map/expert_sum/pallas_call | solution.py:353
  77.2 5.3 %collective-permute-start.19 = (bf16[128,1536]{1,0:T(8,128)(2,1)S(1)}, bf16[128,1536]{1,0:T(8,128)(2,1)S(1)}, u32[]{:S(2)}, u32[]{:S(2)}) collective-permute-start(bf16[128,1536]{1,0:T(8,128)(2,1)S(1)} %payload.20.refs_0_), channel_id=1, source_target_pairs={{0,2},{1,3},{2,0},{3,1},{4,6},{5,7},{6,4},{7,5},{8,10},{9,11},{10,... | collective-permute-start | bytes 1179656 | tf_op jit(solution)/shard_map/ppermute | solution.py:442
  84.8 2.7 %expert_sum.9.refs_0_.for_outer.other = bf16[128,1536]{1,0:T(8,128)(2,1)S(1)} custom-call(s32[73]{0:T(128)S(1)} %get-tuple-element.29.refs_0_.numbers, bf16[128,1536]{1,0:T(8,128)(2,1)S(1)} %collective-permute-done.20.near.one, bf16[128,1536]{1,0:T(8,128)(2,1)S(1)} %collective-permute-done.18.for_inner.far, f32[4,256,8]{2,1,0:T(8,128)S(1)} %get-tuple-element.44.named, ...), custom_call_target="tpu_custom_call" | custom-call | flops 1811939328 | bytes 14999844 | tf_op jit(solution)/shard_map/expert_sum/pallas_call | solution.py:353
  87.5 3.8 %collective-permute-done.19.one.near = bf16[128,1536]{1,0:T(8,128)(2,1)S(1)} collective-permute-done((bf16[128,1536]{1,0:T(8,128)(2,1)S(1)}, bf16[128,1536]{1,0:T(8,128)(2,1)S(1)}, u32[]{:S(2)}, u32[]{:S(2)}) %collective-permute-start.19) | collective-permute-done | bytes 393248 | tf_op jit(solution)/shard_map/ppermute | solution.py:442
  93.7 2.9 %expert_sum.10.other.refs_0_ = bf16[128,1536]{1,0:T(8,128)(2,1)S(1)} custom-call(s32[73]{0:T(128)S(1)} %get-tuple-element.29.refs_0_.numbers, bf16[128,1536]{1,0:T(8,128)(2,1)S(1)} %collective-permute-done.19.one.near, bf16[128,1536]{1,0:T(8,128)(2,1)S(1)} %collective-permute-done.12.near.for_outer.for_inner.far, f32[4,256,8]{2,1,0:T(8,128)S(1)} %get-tuple-element.44.named, ...), custom_call_target="tpu_custom_call" | custom-call | flops 1811939328 | bytes 14999844 | tf_op jit(solution)/shard_map/expert_sum/pallas_call | solution.py:353
  96.7 4.9 %collective-permute-start.22 = (bf16[128,1536]{1,0:T(8,128)(2,1)S(1)}, bf16[128,1536]{1,0:T(8,128)(2,1)S(1)}, u32[]{:S(2)}, u32[]{:S(2)}) collective-permute-start(bf16[128,1536]{1,0:T(8,128)(2,1)S(1)} %payload.23.refs_0_), channel_id=1, source_target_pairs={{0,2},{1,3},{2,0},{3,1},{4,6},{5,7},{6,4},{7,5},{8,10},{9,11},{10,... | collective-permute-start | bytes 1179656 | tf_op jit(solution)/shard_map/ppermute | solution.py:442
  103.9 2.7 %expert_sum.11.refs_0_.other = bf16[128,1536]{1,0:T(8,128)(2,1)S(1)} custom-call(s32[73]{0:T(128)S(1)} %get-tuple-element.29.refs_0_.numbers, bf16[128,1536]{1,0:T(8,128)(2,1)S(1)} %collective-permute-done.24.one.near, bf16[128,1536]{1,0:T(8,128)(2,1)S(1)} %collective-permute-done.16.for_outer.for_inner.near.far, f32[4,256,8]{2,1,0:T(8,128)S(1)} %get-tuple-element.44.named, ...), custom_call_target="tpu_custom_call" | custom-call | flops 1811939328 | bytes 14999844 | tf_op jit(solution)/shard_map/expert_sum/pallas_call | solution.py:353
  106.6 5.1 %collective-permute-done.22.for_outer.one = bf16[128,1536]{1,0:T(8,128)(2,1)S(1)} collective-permute-done((bf16[128,1536]{1,0:T(8,128)(2,1)S(1)}, bf16[128,1536]{1,0:T(8,128)(2,1)S(1)}, u32[]{:S(2)}, u32[]{:S(2)}) %collective-permute-start.22) | collective-permute-done | bytes 393248 | tf_op jit(solution)/shard_map/ppermute | solution.py:442
  114.0 4.7 %own_sum.1 = (bf16[128,1536]{1,0:T(8,128)(2,1)S(1)}, f32[128,1536]{1,0:T(8,128)S(1)}) custom-call(s32[73]{0:T(128)S(1)} %get-tuple-element.29.refs_0_.numbers, bf16[128,1536]{1,0:T(8,128)(2,1)S(1)} %get-tuple-element.38.first, bf16[128,1536]{1,0:T(8,128)(2,1)S(1)} %get-tuple-element.43.refs_0_.for_outer.for_inner.second, ...), custom_call_target="tpu_custom_call" | custom-call | flops 3623878656 | bytes 16965924 | tf_op jit(solution)/shard_map/own_sum/pallas_call | solution.py:353
  118.7 4.1 %collective-permute-done.26 = bf16[128,1536]{1,0:T(8,128)(2,1)S(1)} collective-permute-done((bf16[128,1536]{1,0:T(8,128)(2,1)S(1)}, bf16[128,1536]{1,0:T(8,128)(2,1)S(1)}, u32[]{:S(2)}, u32[]{:S(2)}) %collective-permute-start.26) | collective-permute-done | bytes 393248 | tf_op jit(solution)/shard_map/ppermute | solution.py:442
  (93 shorter events, 24.1 us)
Async XLA Ops:
  0.0 32.4 %collective-permute-start.3 = (bf16[1,1536,1536]{2,1,0:T(8,128)(2,1)}, bf16[1,1536,1536]{2,1,0:T(8,128)(2,1)}, u32[]{:S(2)}, u32[]{:S(2)}) collective-permute-start(bf16[1,1536,1536]{2,1,0:T(8,128)(2,1)} %param.36), channel_id=1, source_target_pairs={{0,1},{1,0},{2,3},{3,2},{4,5},{5,4},{6,7},{7,6},{8,9},{9,8},{10,11... | collective-permute-start | bytes 14155784 | tf_op jit(solution)/shard_map/ppermute | solution.py:442
  0.5 31.9 %collective-permute-start.4 = (bf16[1,768,1536]{2,1,0:T(8,128)(2,1)}, bf16[1,768,1536]{2,1,0:T(8,128)(2,1)S(1)}, u32[]{:S(2)}, u32[]{:S(2)}) collective-permute-start(bf16[1,768,1536]{2,1,0:T(8,128)(2,1)} %param.37), channel_id=1, source_target_pairs={{0,1},{1,0},{2,3},{3,2},{4,5},{5,4},{6,7},{7,6},{8,9},{9,8},{10,11... | collective-permute-start | bytes 7077896 | tf_op jit(solution)/shard_map/ppermute | solution.py:442
  2.1 11.3 %collective-permute-start.2 = (bf16[5,16,512]{2,1,0:T(8,128)(2,1)S(1)}, bf16[5,16,512]{2,1,0:T(8,128)(2,1)S(1)}, u32[]{:S(2)}, u32[]{:S(2)}) collective-permute-start(bf16[5,16,512]{2,1,0:T(8,128)(2,1)S(1)} %pad_maximum_fusion.2.refs_7_), channel_id=1, source_target_pairs={{0,6},{1,7},{2,4},{3,5},{4,2},{5,3},{6,0},{7,1},{8,14},{9,15},{10,... | collective-permute-start | bytes 245768 | tf_op jit(solution)/shard_map/ppermute | solution.py:442
  7.2 7.0 %collective-permute-start.1 = (bf16[5,16,512]{2,1,0:T(8,128)(2,1)S(1)}, bf16[5,16,512]{2,1,0:T(8,128)(2,1)S(1)}, u32[]{:S(2)}, u32[]{:S(2)}) collective-permute-start(bf16[5,16,512]{2,1,0:T(8,128)(2,1)S(1)} %pad_maximum_fusion.2.refs_7_), channel_id=1, source_target_pairs={{0,4},{1,5},{2,6},{3,7},{4,0},{5,1},{6,2},{7,3},{8,12},{9,13},{10,... | collective-permute-start | bytes 245768 | tf_op jit(solution)/shard_map/ppermute | solution.py:442
  7.2 7.0 %collective-permute-start = (bf16[5,16,512]{2,1,0:T(8,128)(2,1)S(1)}, bf16[5,16,512]{2,1,0:T(8,128)(2,1)S(1)}, u32[]{:S(2)}, u32[]{:S(2)}) collective-permute-start(bf16[5,16,512]{2,1,0:T(8,128)(2,1)S(1)} %pad_maximum_fusion.2.refs_7_), channel_id=1, source_target_pairs={{0,2},{1,3},{2,0},{3,1},{4,6},{5,7},{6,4},{7,5},{8,10},{9,11},{10,... | collective-permute-start | bytes 245768 | tf_op jit(solution)/shard_map/ppermute | solution.py:442
  15.1 11.7 %collective-permute-start.7 = (bf16[16,16,512]{2,1,0:T(8,128)(2,1)S(1)}, bf16[16,16,512]{2,1,0:T(8,128)(2,1)S(1)}, u32[]{:S(2)}, u32[]{:S(2)}) collective-permute-start(bf16[16,16,512]{2,1,0:T(8,128)(2,1)S(1)} %after.2.refs_0_), channel_id=1, source_target_pairs={{0,24},{8,16},{16,8},{24,0},{1,25},{9,17},{17,9},{25,1},{2,26},{10... | collective-permute-start | bytes 786440 | tf_op jit(solution)/shard_map/ppermute | solution.py:442
  17.6 11.6 %collective-permute-start.6 = (bf16[16,16,512]{2,1,0:T(8,128)(2,1)S(1)}, bf16[16,16,512]{2,1,0:T(8,128)(2,1)S(1)}, u32[]{:S(2)}, u32[]{:S(2)}) collective-permute-start(bf16[16,16,512]{2,1,0:T(8,128)(2,1)S(1)} %after.2.refs_0_), channel_id=1, source_target_pairs={{0,16},{8,24},{16,0},{24,8},{1,17},{9,25},{17,1},{25,9},{2,18},{10... | collective-permute-start | bytes 786440 | tf_op jit(solution)/shard_map/ppermute | solution.py:442
  18.1 11.2 %collective-permute-start.5 = (bf16[16,16,512]{2,1,0:T(8,128)(2,1)S(1)}, bf16[16,16,512]{2,1,0:T(8,128)(2,1)S(1)}, u32[]{:S(2)}, u32[]{:S(2)}) collective-permute-start(bf16[16,16,512]{2,1,0:T(8,128)(2,1)S(1)} %after.2.refs_0_), channel_id=1, source_target_pairs={{0,8},{8,0},{16,24},{24,16},{1,9},{9,1},{17,25},{25,17},{2,10},{10... | collective-permute-start | bytes 786440 | tf_op jit(solution)/shard_map/ppermute | solution.py:442
  39.4 10.5 %collective-permute-start.12 = (bf16[128,1536]{1,0:T(8,128)(2,1)S(1)}, bf16[128,1536]{1,0:T(8,128)(2,1)S(1)}, u32[]{:S(2)}, u32[]{:S(2)}) collective-permute-start(bf16[128,1536]{1,0:T(8,128)(2,1)S(1)} %get-tuple-element.38.first), channel_id=1, source_target_pairs={{0,2},{1,3},{2,0},{3,1},{4,6},{5,7},{6,4},{7,5},{8,10},{9,11},{10,... | collective-permute-start | bytes 1179656 | tf_op jit(solution)/shard_map/ppermute | solution.py:442
  40.2 9.9 %collective-permute-start.13 = (bf16[128,1536]{1,0:T(8,128)(2,1)S(1)}, bf16[128,1536]{1,0:T(8,128)(2,1)S(1)}, u32[]{:S(2)}, u32[]{:S(2)}) collective-permute-start(bf16[128,1536]{1,0:T(8,128)(2,1)S(1)} %get-tuple-element.38.first), channel_id=1, source_target_pairs={{0,1},{1,0},{2,4},{3,5},{4,2},{5,3},{6,7},{7,6},{8,9},{9,8},{10,12... | collective-permute-start | bytes 1179656 | tf_op jit(solution)/shard_map/ppermute | solution.py:532
  50.0 5.7 %collective-permute-start.14 = (bf16[128,1536]{1,0:T(8,128)(2,1)S(1)}, bf16[128,1536]{1,0:T(8,128)(2,1)S(1)}, u32[]{:S(2)}, u32[]{:S(2)}) collective-permute-start(bf16[128,1536]{1,0:T(8,128)(2,1)S(1)} %payload.15.refs_0_), channel_id=1, source_target_pairs={{0,1},{1,0},{2,4},{3,5},{4,2},{5,3},{6,7},{7,6},{8,9},{9,8},{10,12... | collective-permute-start | bytes 1179656 | tf_op jit(solution)/shard_map/ppermute | solution.py:528
  50.2 12.1 %collective-permute-start.16 = (bf16[128,1536]{1,0:T(8,128)(2,1)S(1)}, bf16[128,1536]{1,0:T(8,128)(2,1)S(1)}, u32[]{:S(2)}, u32[]{:S(2)}) collective-permute-start(bf16[128,1536]{1,0:T(8,128)(2,1)S(1)} %payload.17), channel_id=1, source_target_pairs={{0,2},{1,3},{2,0},{3,1},{4,6},{5,7},{6,4},{7,5},{8,10},{9,11},{10,... | collective-permute-start | bytes 1179656 | tf_op jit(solution)/shard_map/ppermute | solution.py:442
  55.8 15.2 %collective-permute-start.15 = (bf16[128,1536]{1,0:T(8,128)(2,1)S(1)}, bf16[128,1536]{1,0:T(8,128)(2,1)S(1)}, u32[]{:S(2)}, u32[]{:S(2)}) collective-permute-start(bf16[128,1536]{1,0:T(8,128)(2,1)S(1)} %payload.16.refs_0_), channel_id=1, source_target_pairs={{0,2},{1,3},{2,0},{3,1},{4,6},{5,7},{6,4},{7,5},{8,10},{9,11},{10,... | collective-permute-start | bytes 1179656 | tf_op jit(solution)/shard_map/ppermute | solution.py:442
  62.4 8.8 %collective-permute-start.17 = (bf16[128,1536]{1,0:T(8,128)(2,1)S(1)}, bf16[128,1536]{1,0:T(8,128)(2,1)S(1)}, u32[]{:S(2)}, u32[]{:S(2)}) collective-permute-start(bf16[128,1536]{1,0:T(8,128)(2,1)S(1)} %payload.18), channel_id=1, source_target_pairs={{0,1},{1,0},{2,4},{3,5},{4,2},{5,3},{6,7},{7,6},{8,9},{9,8},{10,12... | collective-permute-start | bytes 1179656 | tf_op jit(solution)/shard_map/ppermute | solution.py:528
  71.1 6.0 %collective-permute-start.18 = (bf16[128,1536]{1,0:T(8,128)(2,1)S(1)}, bf16[128,1536]{1,0:T(8,128)(2,1)S(1)}, u32[]{:S(2)}, u32[]{:S(2)}) collective-permute-start(bf16[128,1536]{1,0:T(8,128)(2,1)S(1)} %payload.19.refs_0_), channel_id=1, source_target_pairs={{0,1},{1,0},{2,4},{3,5},{4,2},{5,3},{6,7},{7,6},{8,9},{9,8},{10,12... | collective-permute-start | bytes 1179656 | tf_op jit(solution)/shard_map/ppermute | solution.py:528
  71.3 13.2 %collective-permute-start.20 = (bf16[128,1536]{1,0:T(8,128)(2,1)S(1)}, bf16[128,1536]{1,0:T(8,128)(2,1)S(1)}, u32[]{:S(2)}, u32[]{:S(2)}) collective-permute-start(bf16[128,1536]{1,0:T(8,128)(2,1)S(1)} %payload.21), channel_id=1, source_target_pairs={{0,2},{1,3},{2,0},{3,1},{4,6},{5,7},{6,4},{7,5},{8,10},{9,11},{10,... | collective-permute-start | bytes 1179656 | tf_op jit(solution)/shard_map/ppermute | solution.py:442
  77.2 14.0 %collective-permute-start.19 = (bf16[128,1536]{1,0:T(8,128)(2,1)S(1)}, bf16[128,1536]{1,0:T(8,128)(2,1)S(1)}, u32[]{:S(2)}, u32[]{:S(2)}) collective-permute-start(bf16[128,1536]{1,0:T(8,128)(2,1)S(1)} %payload.20.refs_0_), channel_id=1, source_target_pairs={{0,2},{1,3},{2,0},{3,1},{4,6},{5,7},{6,4},{7,5},{8,10},{9,11},{10,... | collective-permute-start | bytes 1179656 | tf_op jit(solution)/shard_map/ppermute | solution.py:442
  84.7 6.8 %collective-permute-start.23 = (bf16[128,1536]{1,0:T(8,128)(2,1)S(1)}, bf16[128,1536]{1,0:T(8,128)(2,1)S(1)}, u32[]{:S(2)}, u32[]{:S(2)}) collective-permute-start(bf16[128,1536]{1,0:T(8,128)(2,1)S(1)} %payload.25), channel_id=1, source_target_pairs={{0,1},{1,0},{2,4},{3,5},{4,2},{5,3},{6,7},{7,6},{8,9},{9,8},{10,12... | collective-permute-start | bytes 1179656 | tf_op jit(solution)/shard_map/ppermute | solution.py:528
  91.5 5.1 %collective-permute-start.21 = (bf16[128,1536]{1,0:T(8,128)(2,1)S(1)}, bf16[128,1536]{1,0:T(8,128)(2,1)S(1)}, u32[]{:S(2)}, u32[]{:S(2)}) collective-permute-start(bf16[128,1536]{1,0:T(8,128)(2,1)S(1)} %payload.22.refs_1_), channel_id=1, source_target_pairs={{0,1},{1,0},{2,4},{3,5},{4,2},{5,3},{6,7},{7,6},{8,9},{9,8},{10,12... | collective-permute-start | bytes 1179656 | tf_op jit(solution)/shard_map/ppermute | solution.py:528
  91.7 12.0 %collective-permute-start.24 = (bf16[128,1536]{1,0:T(8,128)(2,1)S(1)}, bf16[128,1536]{1,0:T(8,128)(2,1)S(1)}, u32[]{:S(2)}, u32[]{:S(2)}) collective-permute-start(bf16[128,1536]{1,0:T(8,128)(2,1)S(1)} %payload.26), channel_id=1, source_target_pairs={{0,2},{1,3},{2,0},{3,1},{4,6},{5,7},{6,4},{7,5},{8,10},{9,11},{10,... | collective-permute-start | bytes 1179656 | tf_op jit(solution)/shard_map/ppermute | solution.py:442
  96.7 14.9 %collective-permute-start.22 = (bf16[128,1536]{1,0:T(8,128)(2,1)S(1)}, bf16[128,1536]{1,0:T(8,128)(2,1)S(1)}, u32[]{:S(2)}, u32[]{:S(2)}) collective-permute-start(bf16[128,1536]{1,0:T(8,128)(2,1)S(1)} %payload.23.refs_0_), channel_id=1, source_target_pairs={{0,2},{1,3},{2,0},{3,1},{4,6},{5,7},{6,4},{7,5},{8,10},{9,11},{10,... | collective-permute-start | bytes 1179656 | tf_op jit(solution)/shard_map/ppermute | solution.py:442
  103.8 8.0 %collective-permute-start.25 = (bf16[128,1536]{1,0:T(8,128)(2,1)S(1)}, bf16[128,1536]{1,0:T(8,128)(2,1)S(1)}, u32[]{:S(2)}, u32[]{:S(2)}) collective-permute-start(bf16[128,1536]{1,0:T(8,128)(2,1)S(1)} %payload.27), channel_id=1, source_target_pairs={{0,1},{1,0},{2,4},{3,5},{4,2},{5,3},{6,7},{7,6},{8,9},{9,8},{10,12... | collective-permute-start | bytes 1179656 | tf_op jit(solution)/shard_map/ppermute | solution.py:528
  112.0 10.8 %collective-permute-start.26 = (bf16[128,1536]{1,0:T(8,128)(2,1)S(1)}, bf16[128,1536]{1,0:T(8,128)(2,1)S(1)}, u32[]{:S(2)}, u32[]{:S(2)}) collective-permute-start(bf16[128,1536]{1,0:T(8,128)(2,1)S(1)} %payload.29.refs_8_), channel_id=1, source_target_pairs={{0,2},{1,3},{2,0},{3,1},{4,6},{5,7},{6,4},{7,5},{8,10},{9,11},{10,... | collective-permute-start | bytes 1179656 | tf_op jit(solution)/shard_map/ppermute | solution.py:442
  113.9 8.8 %collective-permute-start.27 = (bf16[128,1536]{1,0:T(8,128)(2,1)S(1)}, bf16[128,1536]{1,0:T(8,128)(2,1)S(1)}, u32[]{:S(2)}, u32[]{:S(2)}) collective-permute-start(bf16[128,1536]{1,0:T(8,128)(2,1)S(1)} %payload.28.refs_0_), channel_id=1, source_target_pairs={{0,1},{1,0},{2,4},{3,5},{4,2},{5,3},{6,7},{7,6},{8,9},{9,8},{10,12... | collective-permute-start | bytes 1179656 | tf_op jit(solution)/shard_map/ppermute | solution.py:528
  (15 other events, 82.6 us)
